TPU v7x, 128 devices: a whole 4x4x4 slice. The times are simulated.
128 devices in a mesh: seq: 64 (over x_lo, z, y, core), tp: 2 (over x_hi).
Axes of the slice: x: 4 (x_hi: 2, x_lo: 2; x = x_hi * 2 + x_lo), y: 4, z: 4, core: 2. Of those that a mesh axis runs over, the one named last changes fastest.
Arguments:
- tokens: bfloat16 [8192, 2048], P('seq'), may hold values from -6 to 6
- doc_lengths: int32 [2, 4], replicated, may hold values from 1 to 4000, as said below
- attn_gain: bfloat16 [2048], P('seq'), may hold values from 0.5 to 1.5
- q_weight: bfloat16 [2048, 2048], P('seq', 'tp'), may hold values from -0.125 to 0.125
- kv_weight: bfloat16 [2048, 256], P('seq'), may hold values from -0.125 to 0.125
- out_weight: bfloat16 [2048, 2048], P('tp', 'seq'), may hold values from -0.5 to 0.5
- ffn_gain: bfloat16 [2048], P('seq'), may hold values from 0.5 to 1.5
- gate_weight: bfloat16 [2048, 5632], P('seq', 'tp'), may hold values from -0.125 to 0.125
- up_weight: bfloat16 [2048, 5632], P('seq', 'tp'), may hold values from -0.125 to 0.125
- down_weight: bfloat16 [5632, 2048], P('tp', 'seq'), may hold values from -0.078125 to 0.078125
- second_queries: bfloat16 [8192, 2048], P('seq', 'tp'), may hold values from -8 to 8
- out_cotangent: bfloat16 [8192, 2048], P('seq'), may hold values from -6 to 6
- second_cotangent: bfloat16 [8192, 2048], P('seq', 'tp'), may hold values from -6 to 6
Outputs:
- result: float32 [8192, 2048], P('seq')
- second_out: float32 [8192, 2048], P('seq', 'tp')
- tokens_grad: float32 [8192, 2048], P('seq')
- attn_gain_grad: float32 [2048], P('seq')
- q_weight_grad: float32 [2048, 2048], P('seq', 'tp')
- kv_weight_grad: float32 [2048, 256], P('seq')
- out_weight_grad: float32 [2048, 2048], P('tp', 'seq')
- ffn_gain_grad: float32 [2048], P('seq')
- gate_weight_grad: float32 [2048, 5632], P('seq', 'tp')
- up_weight_grad: float32 [2048, 5632], P('seq', 'tp')
- down_weight_grad: float32 [5632, 2048], P('tp', 'seq')
- second_queries_grad: float32 [8192, 2048], P('seq', 'tp')
Inputs may be any that keep to these rules, and one draw needn't show every extreme that they name: `doc_lengths`: each row sums to 4096. In each row one document, at a place drawn from the seed, has exactly 4096 - 3 * (32) tokens; the other documents of the row together have (3) * (32) tokens, and one of them has exactly 1.
All inputs are finite; a program needn't handle non-finite values.
Results may differ from a plain program's by a relative error of at most 0.018.
Values may be sent and summed in bfloat16 or wider, within the bound.
No kernel may reach another device: no remote copies, remote signals or barrier semaphores. Data moves between devices by JAX's collectives and lax.ppermute only.
A program may use at most 256 MiB of HBM per device.

v0:
```python
import functools
import math

import jax
import jax.numpy as jnp
from jax import lax
from jax.experimental import pallas as pl
from jax.experimental.pallas import tpu as pltpu
from jax.sharding import Mesh, PartitionSpec as P

norm_eps = 1e-05
rope_base = 10000.0
masked_fill = -1e30
KEY_BLOCK = 1024
BF = jnp.bfloat16
F32 = jnp.float32
MB = 1024 * 1024


def fetch(block, axis, offset):
    n = lax.axis_size(axis)
    return lax.ppermute(block, axis, [((i + offset) % n, i) for i in range(n)])


def hand(block, axis, offset):
    return fetch(block, axis, -offset)


def in_order(first, mine, other, axis):
    return jnp.where(
        first,
        jnp.concatenate([mine, other], axis=axis),
        jnp.concatenate([other, mine], axis=axis),
    )


X, Z, Y, CORE = 0, 1, 2, 3


def near_blocks(pair):
    return [fetch(block, axis, d) for block, axis in pair for d in (1, 3)]


def far_blocks(pair, near):
    out = []
    for i, (block, axis) in enumerate(pair):
        after, before = near[2 * i : 2 * i + 2]
        half = block.shape[0] // 2
        far = (fetch(after[:half], axis, 1), fetch(before[half:], axis, 3))
        out.append([block, after, far, before])
    return out[0] + out[1]


def across_x(mine, other):
    rows = mine.shape[0]
    got = fetch(jnp.concatenate([mine, other], axis=0), "x", 1)
    return [
        jnp.concatenate([mine, got[:rows]], axis=0),
        jnp.concatenate([other, got[rows:]], axis=0),
    ]


def first_blocks(pieces):
    return [
        [piece] + [fetch(piece, axis, d) for d in (1, 2, 3)] for piece, axis in zip(pieces, ("z", "y"))
    ]


def second_pair(halves):
    return [(halves[0], "y"), (halves[1], "z")]


def place_in_chunks(pos_ref, x, z, y, dh):
    dx = lax.rem(x - pos_ref[X] + 2, 2)
    dz = lax.rem(z - pos_ref[Z] + 4, 4)
    dy = lax.rem(y - pos_ref[Y] + 4, 4)
    own = dh == 0
    return dh * 4 + jnp.where(own, dy, dz), jnp.where(own, dz, dy) * 2 + dx


def group_place(pos_ref, group):
    h, y, z, x = group % 2, group // 2 % 4, group // 8 % 4, group // 32
    return place_in_chunks(pos_ref, x, z, y, lax.rem(h + pos_ref[CORE], 2))


def whole_place(pos_ref, group):
    h, y, z, x = group % 2, group // 2 % 4, group // 8 % 4, group // 32
    dx = lax.rem(x - pos_ref[X] + 2, 2)
    return (z * 4 + y) * 4 + dx * 2 + lax.rem(h + pos_ref[CORE], 2)


SMEM_SPEC = pl.BlockSpec(memory_space=pltpu.SMEM)
VMEM_SPEC = pl.BlockSpec(memory_space=pltpu.VMEM)
ANY_SPEC = pl.BlockSpec(memory_space=pl.ANY)
SMALL = pl.CostEstimate(flops=1024, bytes_accessed=1024, transcendentals=0)


def call(kernel, name, in_specs, out_specs, out_shape, scratch=(), limit=24, grid=None, **more):
    return pl.pallas_call(
        kernel,
        grid=grid or (1,),
        in_specs=in_specs,
        out_specs=out_specs,
        out_shape=out_shape,
        scratch_shapes=scratch,
        compiler_params=pltpu.CompilerParams(vmem_limit_bytes=limit * MB),
        cost_estimate=SMALL,
        name=name,
        **more,
    )


def tie(*arrays):
    return list(lax.optimization_barrier(arrays))


def both_cores(pos_ref, own, other):
    first = pos_ref[CORE] == 0
    return jnp.concatenate(
        [jnp.where(first, own, other), jnp.where(first, other, own)], axis=0
    )


def turn(pos_ref, act_ref, out_ref, place=group_place):
    for block in range(16):
        part = act_ref[:, block * 128 : (block + 1) * 128].T
        for k in range(4):
            out_ref[place(pos_ref, block * 4 + k)] = part[k * 32 : (k + 1) * 32]


def turned(pos, own, other, whole=False):
    toks, feats = own.shape
    shape = (64, 32, 2 * toks) if whole else (8, 8, 32, 2 * toks)

    def kernel(pos_ref, own_ref, other_ref, out_ref, act):
        act[...] = both_cores(pos_ref, own_ref[...], other_ref[...])
        turn(pos_ref, act, out_ref, whole_place if whole else group_place)

    out = call(
        kernel,
        "turned",
        [SMEM_SPEC, VMEM_SPEC, VMEM_SPEC],
        VMEM_SPEC,
        jax.ShapeDtypeStruct(shape, own.dtype),
        [pltpu.VMEM((2 * toks, feats), own.dtype)],
    )(pos, own, other)
    return out.reshape((2048, 2 * toks) if whole else (8, 256, 2 * toks))


def normed_rows(pos, own, other, chunks, width, at):
    toks, feats = own.shape

    def kernel(pos_ref, own_ref, other_ref, *refs):
        sides, gains, (out_ref, gain_ref, side_ref, wide, act) = refs[:8], refs[8:16], refs[16:]
        for k in range(8):
            wide[k] = gains[k][...].astype(F32).reshape(8, 32, 128)
        for block in range(feats // 128):
            groups = [wide[group_place(pos_ref, block * 4 + k)] for k in range(4)]
            gain_ref[:, block * 128 : (block + 1) * 128] = jnp.concatenate(groups, axis=0).T[:8]
        rows = both_cores(pos_ref, own_ref[...], other_ref[...]).astype(F32)
        inverse = lax.rsqrt(jnp.mean(rows * rows, axis=-1, keepdims=True) + norm_eps)
        act[...] = (rows * inverse * gain_ref[0:1, :]).astype(BF)
        turn(pos_ref, act, out_ref)
        total = jnp.zeros((2 * toks, width), F32)
        for k in range(8):
            turned_rows = out_ref[k].reshape(256, 2 * toks)
            total = total + jnp.dot(turned_rows.T, sides[k][...], preferred_element_type=F32)
        side_ref[...] = total

    specs = [pl.BlockSpec((256, w), lambda i, b=b: (0, b)) for w, b in ((width, at), (128, at + 1))]
    out, gains, side = call(
        kernel,
        "normed_rows",
        [SMEM_SPEC] + [VMEM_SPEC] * 2 + [specs[0]] * 8 + [specs[1]] * 8,
        [VMEM_SPEC] * 3,
        [
            jax.ShapeDtypeStruct((8, 8, 32, 2 * toks), BF),
            jax.ShapeDtypeStruct((8, feats), F32),
            jax.ShapeDtypeStruct((2 * toks, width), F32),
        ],
        [pltpu.VMEM((8, 8, 32, 128), F32), pltpu.VMEM((2 * toks, feats), BF)],
    )(pos, own, other, *chunks, *chunks)
    return out.reshape(8, 256, 2 * toks), gains, side


def turn_back(pos_ref, wide_ref, own_ref, other_ref, place=group_place):
    first = pos_ref[CORE] == 0
    half = wide_ref.shape[-1] // 2
    for block in range(16):
        groups = [wide_ref[place(pos_ref, block * 4 + k)] for k in range(4)]
        rows = jnp.concatenate(groups, axis=0).T.astype(own_ref.dtype)
        at = slice(block * 128, (block + 1) * 128)
        own_ref[:, at] = jnp.where(first, rows[:half], rows[half:])
        other_ref[:, at] = jnp.where(first, rows[half:], rows[:half])


def project(act, chunks, width, at, kind):
    toks = act.shape[-1]

    def kernel(act_ref, *refs):
        weights, out = refs[:8], refs[8]
        total = jnp.zeros((toks, width), F32)
        for k in range(8):
            total = total + jnp.dot(
                act_ref[k].T, weights[k][...], preferred_element_type=F32
            )
        out[...] = total.T.astype(kind)

    return call(
        kernel,
        "project",
        [VMEM_SPEC] + [pl.BlockSpec((256, width), lambda i: (0, at))] * 8,
        VMEM_SPEC,
        jax.ShapeDtypeStruct((width, toks), kind),
    )(act, *chunks)


def unproject(pos, sides):
    count = len(sides)
    toks = sides[0][2].shape[0 if sides[0][3] else 1]
    operands, specs, starts = [], [], []
    for chunks, at, side, flipped in sides:
        width = side.shape[1 if flipped else 0]
        starts.append(len(operands))
        if isinstance(chunks, list):
            operands += chunks
            specs += [pl.BlockSpec((256, width), lambda i, at=at: (0, at))] * 8
        else:
            operands.append(chunks)
            specs.append(VMEM_SPEC)

    def kernel(pos_ref, *refs):
        rights, weights = refs[:count], refs[count : count + len(operands)]
        own_ref, other_ref, wide = refs[count + len(operands) :]
        for k in range(8):
            total = None
            for i, (chunks, at, side, flipped) in enumerate(sides):
                begin = starts[i]
                left = weights[begin + k][...] if isinstance(chunks, list) else weights[begin][k]
                dims = (((1,), (1 if flipped else 0,)), ((), ()))
                part = lax.dot_general(left, rights[i][...], dims, preferred_element_type=F32)
                total = part if total is None else total + part
            wide[k] = total.reshape(8, 32, toks)
        turn_back(pos_ref, wide, own_ref, other_ref)

    return call(
        kernel,
        "unproject",
        [SMEM_SPEC] + [VMEM_SPEC] * count + specs,
        [VMEM_SPEC] * 2,
        [jax.ShapeDtypeStruct((toks // 2, 2048), BF)] * 2,
        [pltpu.VMEM((8, 8, 32, toks), F32)],
    )(pos, *[side[2] for side in sides], *operands)


TILE = 256


def tile_columns(hidden):
    return [(3 * at, at, min(TILE, hidden - at)) for at in range(0, hidden, TILE)]


def feed_forward(pos, normed2, cot, weights):
    toks = normed2.shape[1]
    width = weights.shape[1]
    hidden_units = width // 3
    tiles = tile_columns(hidden_units)

    def kernel(pos_ref, normed_ref, cot_ref, w_ref, grad_ref, *refs):
        d_norm_refs, ffn_refs = refs[:2], refs[2:4]
        normed_rows, cot_rows, pair_weights, down_weights, pair_side, hidden_side, wide = refs[4:]
        j = pl.program_id(0)

        @pl.when(j == 0)
        def _():
            for k in range(8):
                at = slice(k * 256, (k + 1) * 256)
                normed_rows[:, at] = normed_ref[at, :].T
                cot_rows[:, at] = cot_ref[at, :].T

        def tile_step(t, begin):
            pre = jnp.dot(normed_rows[...], w_ref[:, : 2 * t], preferred_element_type=F32)
            d_hidden = jnp.dot(
                cot_rows[...], w_ref[:, 2 * t : 3 * t], preferred_element_type=F32
            )
            gate, up = pre[:, :t], pre[:, t:]
            gate_sig = jax.nn.sigmoid(gate)
            gate_act = gate * gate_sig
            hidden = (gate_act * up).astype(BF)
            d_gate = (d_hidden * up * gate_sig * (1.0 + gate * (1.0 - gate_sig))).astype(BF)
            d_up = (d_hidden * gate_act).astype(BF)
            d_pair = jnp.concatenate([d_gate, d_up], axis=1)
            grad_ref[:, : 2 * t] = jnp.dot(
                normed_ref[...], d_pair, preferred_element_type=F32
            ).astype(BF)
            grad_ref[:, 2 * t : 3 * t] = jnp.dot(
                cot_ref[...], hidden, preferred_element_type=F32
            ).astype(BF)
            pair_at, down_at = pl.ds(2 * begin, 2 * t), pl.ds(begin, t)
            pair_side[:, pair_at] = d_pair
            hidden_side[:, down_at] = hidden
            pair_weights[:, pair_at] = w_ref[:, : 2 * t]
            down_weights[:, down_at] = w_ref[:, 2 * t : 3 * t]

        last = tiles[-1]

        @pl.when(j < len(tiles) - 1)
        def _():
            tile_step(TILE, pl.multiple_of(j * TILE, TILE))

        @pl.when(j == len(tiles) - 1)
        def _():
            tile_step(last[2], last[1])
            dims = (((1,), (1,)), ((), ()))
            for out_refs, left, right in (
                (d_norm_refs, pair_weights, pair_side),
                (ffn_refs, down_weights, hidden_side),
            ):
                wide[...] = lax.dot_general(
                    left[...], right[...], dims, preferred_element_type=F32
                ).reshape(64, 32, toks)
                turn_back(pos_ref, wide, *out_refs, whole_place)

    whole = pl.BlockSpec((2048, toks), lambda j: (0, 0))
    tile = pl.BlockSpec((2048, 3 * TILE), lambda j: (0, j))
    rows = pl.BlockSpec((toks // 2, 2048), lambda j: (0, 0))
    outs = call(
        kernel,
        "feed_forward",
        [SMEM_SPEC, whole, whole, tile],
        [tile] + [rows] * 4,
        [jax.ShapeDtypeStruct((2048, width), BF)]
        + [jax.ShapeDtypeStruct((toks // 2, 2048), BF)] * 4,
        [
            pltpu.VMEM((toks, 2048), BF),
            pltpu.VMEM((toks, 2048), BF),
            pltpu.VMEM((2048, 2 * hidden_units), BF),
            pltpu.VMEM((2048, hidden_units), BF),
            pltpu.VMEM((toks, 2 * hidden_units), BF),
            pltpu.VMEM((toks, hidden_units), BF),
            pltpu.VMEM((64, 32, toks), F32),
        ],
        limit=60,
        grid=(len(tiles),),
    )(pos, normed2, cot, weights)
    return outs[0], outs[1:3], outs[3:5]


SEND_ORDER = (1, 5, 3, 7, 2, 6, 0, 4)


def weight_chunks(terms):
    widths = [r.shape[0] if f else r.shape[1] for l, r, f in terms]
    total = sum(widths)
    operands = [l for l, r, f in terms] + [r for l, r, f in terms]
    count = len(operands)

    def kernel(*refs):
        ins, outs = refs[:count], refs[count : count + 8]
        slots, sem = refs[-2:]
        copies = []
        for step, chunk in enumerate(SEND_ORDER):
            slot = step % 2
            if step >= 2:
                copies[step - 2].wait()
            begin = 0
            for i, (left, right, flipped) in enumerate(terms):
                dims = (((1,), (1 if flipped else 0,)), ((), ()))
                product = lax.dot_general(
                    ins[i][chunk], ins[len(terms) + i][...], dims, preferred_element_type=F32
                )
                slots[slot, :, begin : begin + widths[i]] = product.astype(BF)
                begin += widths[i]
            copies.append(pltpu.make_async_copy(slots.at[slot], outs[chunk], sem.at[slot]))
            copies[step].start()
        copies[-2].wait()
        copies[-1].wait()

    return call(
        kernel,
        "weight_chunks",
        [VMEM_SPEC] * count,
        [ANY_SPEC] * 8,
        [jax.ShapeDtypeStruct((256, total), BF)] * 8,
        [pltpu.VMEM((2, 256, total), BF), pltpu.SemaphoreType.DMA((2,))],
    )(*operands)


def summed(parts):
    total = parts[0].astype(F32)
    for part in parts[1:]:
        total = total + part.astype(F32)
    return total


def scatter_first(chunks):
    first = []
    for h, axis in ((0, "y"), (1, "z")):
        first += [chunks[4 * h]] + [hand(chunks[4 * h + d], axis, d) for d in (1, 2, 3)]
    return first


def scatter_second(first, beside):
    second = []
    for terms, axis in ((first[:4], "z"), (first[4:], "y")):
        parts = [summed([t[d * 64 : (d + 1) * 64] for t in terms]).astype(BF) for d in range(4)]
        second.append([parts[0]] + [hand(parts[d], axis, d) for d in (1, 2, 3)])
    shares = [summed(terms) for terms in second]
    give = jnp.concatenate([share[32:].astype(BF) for share in shares], axis=0)
    give, beside = tie(give, beside)
    got = fetch(give, "x", 1).astype(F32)
    return shares[0][:32] + got[:32], shares[1][:32] + got[32:], beside


def prepared(pos, q, out_t, kv, gate, up, down_t, gains):
    rows = q.shape[0]
    hidden = gate.shape[1] // 2
    attn_width = (q.shape[1] + out_t.shape[1] + kv.shape[1]) // 2 + 128

    def kernel(pos_ref, q_ref, out_t_ref, kv_ref, gate_ref, up_ref, down_ref, *refs):
        gain_refs, (attn_mine, attn_give, ffn_mine, ffn_give) = refs[:2], refs[2:]
        first = pos_ref[CORE] == 0

        def put(mine_ref, give_ref, to, source, at, width):
            half = source.shape[1] // 2
            one, two = source[:, at : at + width], source[:, half + at : half + at + width]
            mine_ref[:, to : to + width] = jnp.where(first, one, two)
            give_ref[:, to : to + width] = jnp.where(first, two, one)

        begin = 0
        for ref in (q_ref, out_t_ref, kv_ref):
            width = ref.shape[1] // 2
            put(attn_mine, attn_give, begin, ref, 0, width)
            begin += width
        same = lax.broadcasted_iota(jnp.int32, (rows, rows), 0) == lax.broadcasted_iota(
            jnp.int32, (rows, rows), 1
        )
        lane = lax.broadcasted_iota(jnp.int32, (rows, 128), 1)
        block = jnp.zeros((rows, 128), F32)
        for i, ref in enumerate(gain_refs):
            column = jnp.sum(jnp.where(same, ref[...].astype(F32), 0.0), axis=1, keepdims=True)
            block = jnp.where(lane == i, column, block)
        attn_mine[:, begin:] = block.astype(BF)
        attn_give[:, begin:] = block.astype(BF)
        for begin, unit, width in tile_columns(hidden):
            for i, ref in enumerate((gate_ref, up_ref, down_ref)):
                put(ffn_mine, ffn_give, begin + i * width, ref, unit, width)

    return call(
        kernel,
        "prepared",
        [SMEM_SPEC] + [VMEM_SPEC] * 8,
        [VMEM_SPEC] * 4,
        [jax.ShapeDtypeStruct((rows, attn_width), BF)] * 2
        + [jax.ShapeDtypeStruct((rows, 3 * hidden), BF)] * 2,
        limit=60,
    )(pos, q, out_t, kv, gate, up, down_t, *[g.reshape(1, -1) for g in gains])


def unpacked(pos, mine, other, layout):
    rows = mine.shape[0]
    halves = [sum(w for b, w in pieces) for pieces in layout]

    def kernel(pos_ref, mine_ref, other_ref, *outs):
        first = pos_ref[CORE] == 0
        for out, half, pieces in zip(outs, halves, layout):
            to = 0
            for begin, width in pieces:
                one, two = mine_ref[:, begin : begin + width], other_ref[:, begin : begin + width]
                out[:, to : to + width] = jnp.where(first, one, two)
                out[:, half + to : half + to + width] = jnp.where(first, two, one)
                to += width

    return call(
        kernel,
        "unpacked",
        [SMEM_SPEC] + [VMEM_SPEC] * 2,
        [VMEM_SPEC] * len(layout),
        [jax.ShapeDtypeStruct((rows, 2 * half), F32) for half in halves],
    )(pos, mine, other)


def arranged(pos, mine, other):
    count, head_dim = mine.shape
    block = 1024

    def kernel(pos_ref, mine_ref, other_ref, k_ref, v_ref, kt_ref, vt_ref):
        first = pos_ref[CORE] == 0
        one, two = mine_ref[...], other_ref[...]
        keys, values = jnp.where(first, one, two), jnp.where(first, two, one)
        k_ref[...] = keys
        v_ref[...] = values
        kt_ref[...] = keys.T
        vt_ref[...] = values.T

    rows = pl.BlockSpec((block, head_dim), lambda i: (i, 0))
    columns = pl.BlockSpec((head_dim, block), lambda i: (0, i))
    natural = jax.ShapeDtypeStruct((count, head_dim), BF)
    across = jax.ShapeDtypeStruct((head_dim, count), BF)
    return call(
        kernel,
        "arranged",
        [SMEM_SPEC, rows, rows],
        [rows, rows, columns, columns],
        [natural, natural, across, across],
        grid=(count // block,),
    )(pos, mine, other)


def key_gradients(pos, act, d_keyval, tokens, d_own, d_other, ffn_gain):
    toks, width = d_keyval.shape

    def kernel(pos_ref, act_ref, side_ref, tokens_ref, own_ref, other_ref, ffn_ref, out_ref, wide):
        for k in range(8):
            product = jnp.dot(act_ref[k], side_ref[...], preferred_element_type=F32)
            wide[k] = product.reshape(8, 32, width)
        rows = tokens_ref[...].astype(F32)
        inverse = lax.rsqrt(jnp.mean(rows * rows, axis=-1, keepdims=True) + norm_eps)
        d_normed = own_ref[...].astype(F32) + other_ref[...].astype(F32)
        attn_gain = jnp.sum(d_normed * rows * inverse, axis=0, keepdims=True)
        gains = jnp.concatenate(
            [attn_gain, 0.5 * ffn_ref[...], jnp.zeros((126, rows.shape[1]), F32)], axis=0
        )
        for block in range(16):
            groups = [wide[group_place(pos_ref, block * 4 + k)] for k in range(4)]
            at = slice(block * 128, (block + 1) * 128)
            out_ref[at, :width] = jnp.concatenate(groups, axis=0).astype(BF)
            out_ref[at, width:] = gains[:, at].T.astype(BF)

    return call(
        kernel,
        "key_gradients",
        [SMEM_SPEC] + [VMEM_SPEC] * 6,
        VMEM_SPEC,
        jax.ShapeDtypeStruct((2048, width + 128), BF),
        [pltpu.VMEM((8, 8, 32, width), F32)],
    )(pos, act, d_keyval, tokens, d_own, d_other, ffn_gain)


def allowed_keys(begin, count, places, starts):
    shape = (count, places.shape[1])
    key_place = begin + lax.broadcasted_iota(jnp.int32, shape, 0)
    return (key_place <= places) & (key_place >= starts)


def row_places(pos_ref, docs_ref, own, rows):
    half = rows // 2
    base = (pos_ref[Z] * 4 + pos_ref[Y]) * rows + jnp.where(own, pos_ref[CORE] * half, 0)
    lane = lax.broadcasted_iota(jnp.int32, (1, rows), 1)
    places = base + jnp.where(own, lax.rem(lane, half), lane)
    end = start = jnp.int32(0)
    starts = jnp.zeros((1, rows), jnp.int32)
    for j in range(docs_ref.shape[1]):
        length = docs_ref[pos_ref[X], j]
        end = end + length
        start = start + jnp.where(base >= end, length, 0)
        starts = starts + jnp.where(places >= end, length, 0)
    last = base + jnp.where(own, half, rows) - 1
    return places, starts, lax.div(start, KEY_BLOCK), lax.div(last, KEY_BLOCK) + 1


def attend_kernel(pos_ref, docs_ref, qt_ref, k_ref, vt_ref, ot_ref, lse_ref, *, first_set, scale):
    units, head_dim, rows = qt_ref.shape
    own = pl.program_id(0) * units >= first_set
    places, starts, low, high = row_places(pos_ref, docs_ref, own, rows)

    def step(j, carry):
        begin = pl.multiple_of(j * KEY_BLOCK, KEY_BLOCK)
        keys = k_ref[pl.ds(begin, KEY_BLOCK), :]
        values = vt_ref[:, pl.ds(begin, KEY_BLOCK)]
        allowed = allowed_keys(begin, KEY_BLOCK, places, starts)
        out = []
        for u in range(units):
            top, mass, acc = carry[u]
            scores = jnp.dot(keys, qt_ref[u], preferred_element_type=F32)
            scores = jnp.where(allowed, scores, masked_fill)
            new_top = jnp.maximum(top, jnp.max(scores, axis=0, keepdims=True))
            weights = jnp.exp2((scores - new_top) * scale)
            shrink = jnp.exp2((top - new_top) * scale)
            mass = mass * shrink + jnp.sum(weights, axis=0, keepdims=True)
            acc = acc * shrink + jnp.dot(
                values, weights.astype(BF), preferred_element_type=F32
            )
            out.append((new_top, mass, acc))
        return tuple(out)

    start = (
        jnp.full((1, rows), masked_fill, F32),
        jnp.zeros((1, rows), F32),
        jnp.zeros((head_dim, rows), F32),
    )
    done = lax.fori_loop(low, high, step, (start,) * units)
    for u in range(units):
        top, mass, acc = done[u]
        ot_ref[u] = acc / mass
        lse_ref[u] = top * scale + jnp.log2(mass)


def attend(pos, docs, qt, keys, values_t, scale):
    units = 2
    blocks, head_dim, rows = qt.shape
    count = keys.shape[0]
    first_set = blocks // 2
    block = pl.BlockSpec((units, head_dim, rows), lambda i, p, d: (i, 0, 0))
    return pl.pallas_call(
        functools.partial(attend_kernel, first_set=first_set, scale=scale),
        grid_spec=pltpu.PrefetchScalarGridSpec(
            num_scalar_prefetch=2,
            grid=(blocks // units,),
            in_specs=[
                block,
                pl.BlockSpec((count, head_dim), lambda i, p, d: (0, 0)),
                pl.BlockSpec((head_dim, count), lambda i, p, d: (0, 0)),
            ],
            out_specs=[block, pl.BlockSpec((units, 1, rows), lambda i, p, d: (i, 0, 0))],
        ),
        out_shape=[
            jax.ShapeDtypeStruct((blocks, head_dim, rows), F32),
            jax.ShapeDtypeStruct((blocks, 1, rows), F32),
        ],
        compiler_params=pltpu.CompilerParams(vmem_limit_bytes=28 * MB),
        cost_estimate=SMALL,
        name="attend",
    )(pos, docs, qt, keys, values_t)


def attend_back_kernel(
    pos_ref, docs_ref, qt_ref, dot_ref, ot_ref, lse_ref, k_ref, kt_ref, v_ref,
    dqt_ref, mine_ref, give_ref, dk_ref, dv_ref, *, first_set, scale, score_scale,
):
    units, head_dim, rows = qt_ref.shape

    @pl.when(pl.program_id(0) == 0)
    def _():
        dk_ref[...] = jnp.zeros_like(dk_ref)
        dv_ref[...] = jnp.zeros_like(dv_ref)

    own = pl.program_id(0) * units >= first_set
    places, starts, low, high = row_places(pos_ref, docs_ref, own, rows)
    queries = [qt_ref[u].T for u in range(units)]
    d_outs = [dot_ref[u].T for u in range(units)]
    deltas = [
        jnp.sum(dot_ref[u].astype(F32) * ot_ref[u], axis=0, keepdims=True) for u in range(units)
    ]

    def step(j, carry):
        begin = pl.multiple_of(j * KEY_BLOCK, KEY_BLOCK)
        part = pl.ds(begin, KEY_BLOCK)
        allowed = allowed_keys(begin, KEY_BLOCK, places, starts)
        out = []
        d_keys = d_values = None
        for u in range(units):
            scores = jnp.dot(k_ref[part, :], qt_ref[u], preferred_element_type=F32)
            d_probs = jnp.dot(v_ref[part, :], dot_ref[u], preferred_element_type=F32)
            probs = jnp.where(allowed, jnp.exp2(scores * scale - lse_ref[u]), 0.0)
            d_scores = (probs * (d_probs - deltas[u])).astype(BF)
            for_keys = jnp.dot(d_scores, queries[u], preferred_element_type=F32)
            for_values = jnp.dot(probs.astype(BF), d_outs[u], preferred_element_type=F32)
            d_keys = for_keys if u == 0 else d_keys + for_keys
            d_values = for_values if u == 0 else d_values + for_values
            out.append(
                carry[u] + jnp.dot(kt_ref[:, part], d_scores, preferred_element_type=F32)
            )
        dk_ref[part, :] += d_keys
        dv_ref[part, :] += d_values
        return tuple(out)

    start = jnp.zeros((head_dim, rows), F32)
    done = lax.fori_loop(low, high, step, (start,) * units)
    for u in range(units):
        dqt_ref[u] = done[u] * score_scale

    @pl.when(pl.program_id(0) == pl.num_programs(0) - 1)
    def _():
        first = pos_ref[CORE] == 0
        d_keys, d_values = dk_ref[...] * score_scale, dv_ref[...]
        mine_ref[...] = jnp.where(first, d_keys, d_values)
        give_ref[...] = jnp.where(first, d_values, d_keys).astype(BF)


def attend_back(pos, docs, qt, d_out_t, out_t, lse, keys, keys_t, values, scale, score_scale):
    units = 2
    blocks, head_dim, rows = qt.shape
    count = keys.shape[0]
    first_set = blocks // 2
    block = pl.BlockSpec((units, head_dim, rows), lambda i, p, d: (i, 0, 0))
    whole = pl.BlockSpec((count, head_dim), lambda i, p, d: (0, 0))
    return pl.pallas_call(
        functools.partial(
            attend_back_kernel, first_set=first_set, scale=scale, score_scale=score_scale
        ),
        grid_spec=pltpu.PrefetchScalarGridSpec(
            num_scalar_prefetch=2,
            grid=(blocks // units,),
            in_specs=[
                block,
                block,
                block,
                pl.BlockSpec((units, 1, rows), lambda i, p, d: (i, 0, 0)),
                whole,
                pl.BlockSpec((head_dim, count), lambda i, p, d: (0, 0)),
                whole,
            ],
            out_specs=[block, whole, whole],
            scratch_shapes=[pltpu.VMEM((count, head_dim), F32)] * 2,
        ),
        out_shape=[
            jax.ShapeDtypeStruct((blocks, head_dim, rows), F32),
            jax.ShapeDtypeStruct((count, head_dim), F32),
            jax.ShapeDtypeStruct((count, head_dim), BF),
        ],
        compiler_params=pltpu.CompilerParams(vmem_limit_bytes=44 * MB),
        cost_estimate=SMALL,
        name="attend_back",
    )(pos, docs, qt, d_out_t, out_t, lse, keys, keys_t, values)


def doc_starts(lengths, places):
    ends = jnp.cumsum(lengths)
    passed = (places[:, None] >= ends[None, :]).astype(jnp.int32)
    return jnp.sum(passed * lengths[None, :], axis=1)


def rotate_rows(values, cosine, sine):
    half = values.shape[-1] // 2
    one, two = values[..., :half], values[..., half:]
    return jnp.concatenate([one * cosine - two * sine, two * cosine + one * sine], axis=-1)


def rotate_columns(values, cosine, sine):
    half = values.shape[1] // 2
    one, two = values[:, :half], values[:, half:]
    return jnp.concatenate([one * cosine - two * sine, two * cosine + one * sine], axis=1)


def head_blocks(array):
    toks, width = array.shape
    count = width // 256

    def kernel(array_ref, out_ref):
        for b in range(count):
            for i in range(2):
                at = (2 * b + i) * 128
                out_ref[b, :, i * toks : (i + 1) * toks] = array_ref[:, at : at + 128].T

    shape = jax.ShapeDtypeStruct((count, 128, 2 * toks), array.dtype)
    return call(kernel, "head_blocks", [VMEM_SPEC], VMEM_SPEC, shape)(array)


def head_blocks_back(blocks, begin):
    total, head_dim, wide = blocks.shape
    count, toks = total - begin, wide // 2

    def kernel(blocks_ref, out_ref):
        for b in range(count):
            for i in range(2):
                at = (2 * b + i) * 128
                out_ref[:, at : at + 128] = blocks_ref[b, :, i * toks : (i + 1) * toks].T

    shape = jax.ShapeDtypeStruct((toks, count * 256), blocks.dtype)
    spec = pl.BlockSpec((count, head_dim, wide), lambda i: (begin // count, 0, 0))
    return call(kernel, "head_blocks_back", [spec], VMEM_SPEC, shape)(blocks)


def on_device(
    tokens, doc_lengths, attn_gain, q_weight, kv_weight, out_weight, ffn_gain,
    gate_weight, up_weight, down_weight, second_queries, out_cotangent, second_cotangent,
):
    x, z, y, c = (lax.axis_index(a) for a in ("x", "z", "y", "c"))
    first = c == 0
    pos = jnp.stack([x, z, y, c]).astype(jnp.int32)
    toks, width = tokens.shape
    head_dim = kv_weight.shape[1] // 2
    score_scale = head_dim ** (-0.5)
    scale = score_scale * math.log2(math.e)
    rows = q_weight.shape[0]

    def swap(own):
        return fetch(own, "c", 1)

    n_q, n_kv = q_weight.shape[1] // 2, head_dim
    n_out, n_ffn = out_weight.shape[0] // 2, down_weight.shape[0] // 2
    n_attn = n_q + n_out
    at_out, at_kv = n_q // n_out, n_attn // n_kv
    attn_mine, attn_give, ffn_mine, ffn_give = prepared(
        pos, q_weight, out_weight.T, kv_weight, gate_weight, up_weight, down_weight.T,
        (attn_gain, ffn_gain),
    )
    attn_other, ffn_other, tokens_other, cot_other = tie(
        swap(attn_give), swap(ffn_give), swap(tokens), swap(out_cotangent)
    )
    *attn_rows, ffn_mine, ffn_other = tie(*across_x(attn_mine, attn_other), ffn_mine, ffn_other)
    ffn_both = jnp.concatenate([ffn_mine, ffn_other], axis=0)
    blocks = first_blocks(attn_rows)
    ffn_got, *blocks = tie(fetch(ffn_both, "x", 1), *blocks[0], *blocks[1])
    ffn_rows = jnp.concatenate([ffn_both, ffn_got], axis=0)
    ffn_whole = lax.all_gather(ffn_rows, ("z", "y"), axis=0, tiled=True)
    attn_pair = second_pair([jnp.concatenate(b, axis=0) for b in (blocks[:4], blocks[4:])])
    attn_chunks = far_blocks(attn_pair, tie(*near_blocks(attn_pair)))
    attn_chunks = [jnp.concatenate(w, axis=0) if isinstance(w, tuple) else w for w in attn_chunks]
    def over_tp(rows):
        send = rows.astype(BF)
        return send.astype(F32) + fetch(send, "t", 1).astype(F32)

    def reduce_rows(own, other):
        return over_tp(own.astype(F32) + swap(other).astype(F32))

    places = (z * 4 + y) * (2 * toks) + jnp.arange(2 * toks, dtype=jnp.int32)
    starts = doc_starts(jnp.where(x == 0, doc_lengths[0], doc_lengths[1]), places)
    positions = (places - starts).astype(F32)
    inverse_freq = jnp.exp(
        jnp.arange(head_dim // 2, dtype=F32) * (-2.0 * math.log(rope_base) / head_dim)
    )
    angles_t = inverse_freq[:, None] * positions[None, :]
    cos_t, sin_t = jnp.cos(angles_t), jnp.sin(angles_t)

    inputs = tokens.astype(F32)
    inv_attn = lax.rsqrt(jnp.mean(inputs * inputs, axis=-1, keepdims=True) + norm_eps)
    second_t, second_cot_t = head_blocks(second_queries), head_blocks(second_cotangent)
    cot_t = turned(pos, out_cotangent, cot_other, whole=True)
    cos_r, sin_r = cos_t.T, sin_t.T
    normed_t, gain_rows, keyval = normed_rows(pos, tokens, tokens_other, attn_chunks, n_kv, at_kv)
    gain_one, gain_two = gain_rows[0:1], gain_rows[1:2]
    kv_own = jnp.where(first, rotate_rows(keyval, cos_r, sin_r), keyval).astype(BF)
    kv_sent = jnp.broadcast_to(kv_own[None], (16,) + kv_own.shape)
    kv_all = lax.all_to_all(kv_sent, ("z", "y"), 0, 0).reshape(-1, head_dim)
    queries_t = project(normed_t, attn_chunks, n_q, 0, F32)
    query_rot = rotate_columns(queries_t.reshape(-1, head_dim, 2 * toks), cos_t, sin_t).astype(BF)
    keys, values, keys_t, values_t = arranged(pos, kv_all, swap(kv_all))
    query_t = jnp.concatenate([query_rot, second_t], axis=0)
    out_t, lse = attend(pos, doc_lengths, query_t, keys, values_t, scale)
    n_first = query_rot.shape[0]
    second_out = head_blocks_back(out_t, n_first)
    attended_t = out_t[:n_first].reshape(-1, 2 * toks).astype(BF)

    branch = reduce_rows(*unproject(pos, [(attn_chunks, at_out, attended_t, False)]))
    resid = inputs + branch
    inv_ffn = lax.rsqrt(jnp.mean(resid * resid, axis=-1, keepdims=True) + norm_eps)
    normed2 = (resid * inv_ffn * gain_two).astype(BF)
    normed2_t = turned(pos, normed2, swap(normed2), whole=True)
    ffn_grads, d_norm2_part, ffn_part = feed_forward(pos, normed2_t, cot_t, ffn_whole)
    ffn_share = lax.psum_scatter(ffn_grads, ("z", "y"), scatter_dimension=0, tiled=True)
    d_normed2 = reduce_rows(*d_norm2_part)

    scaled_two = gain_two * d_normed2
    ffn_gain_part = jnp.sum(d_normed2 * resid * inv_ffn, axis=0)
    d_resid = (
        out_cotangent.astype(F32)
        + inv_ffn * scaled_two
        - resid * inv_ffn**3 * jnp.mean(scaled_two * resid, axis=-1, keepdims=True)
    )
    d_branch = d_resid.astype(BF)

    d_branch_t = turned(pos, d_branch, swap(d_branch))
    d_attended_t = project(d_branch_t, attn_chunks, n_out, at_out, BF)
    d_out_t = jnp.concatenate(
        [d_attended_t.reshape(-1, head_dim, 2 * toks), second_cot_t], axis=0
    )
    d_query_t, kv_mine, kv_give = attend_back(
        pos, doc_lengths, query_t, d_out_t, out_t, lse, keys, keys_t, values, scale, score_scale
    )
    kv_give, d_query_t, *ffn_part = tie(kv_give, d_query_t, *ffn_part)
    ffn_sum = reduce_rows(*ffn_part)
    kv_other = swap(kv_give)
    second_queries_grad = head_blocks_back(d_query_t, n_first)
    d_queries_t = rotate_columns(d_query_t[:n_first], cos_t, -sin_t).reshape(-1, 2 * toks).astype(BF)

    attn_grads = weight_chunks([(normed_t, d_queries_t, True), (d_branch_t, attended_t, True)])
    kv_chip = (kv_mine + kv_other.astype(F32)).astype(BF).reshape(16, 2 * toks, head_dim)
    kv_chip, *attn_grads = tie(kv_chip, *attn_grads)
    kv_parts = lax.all_to_all(kv_chip, ("z", "y"), 0, 0)
    kv_parts, ffn_sum = tie(kv_parts, ffn_sum)
    kv_sum = jnp.sum(kv_parts.astype(F32), axis=0)
    result = resid + ffn_sum
    d_keyval = jnp.where(first, rotate_rows(kv_sum, cos_r, -sin_r), kv_sum).astype(BF)
    d_norm_part = unproject(
        pos, [(attn_chunks, 0, d_queries_t, False), (attn_chunks, at_kv, d_keyval, True)]
    )
    d_norm_other = swap(d_norm_part[1])
    d_normed = over_tp(d_norm_part[0].astype(F32) + d_norm_other.astype(F32))
    kv_grads = key_gradients(
        pos, normed_t, d_keyval, tokens, d_norm_part[0], d_norm_other, ffn_gain_part[None]
    )
    kv_got = lax.all_to_all(kv_grads.reshape(32, 2, rows, -1), ("x", "z", "y"), 0, 0)
    kv_got, *attn_terms = tie(kv_got, *scatter_first(attn_grads))
    ffn_got = fetch(ffn_share[64:], "x", 1)
    attn_share, attn_give, ffn_got = scatter_second(attn_terms, ffn_got)
    ffn_sums = ffn_share[:64].astype(F32) + ffn_got.astype(F32)
    kv_share = jnp.sum(kv_got.astype(F32), axis=0)
    scaled_one = gain_one * d_normed
    tokens_grad = (
        d_resid
        + inv_attn * scaled_one
        - inputs * inv_attn**3 * jnp.mean(scaled_one * inputs, axis=-1, keepdims=True)
    )

    gate_grad, up_grad, down_grad_t = unpacked(
        pos,
        ffn_sums[:32],
        swap(ffn_sums[32:]),
        [[(b + i * w, w) for b, unit, w in tile_columns(n_ffn)] for i in range(3)],
    )
    q_grad, out_grad_t = unpacked(pos, attn_share, swap(attn_give), [[(0, n_q)], [(n_q, n_out)]])
    kv_mine, kv_give = (jnp.where(first, kv_share[i], kv_share[1 - i]) for i in (0, 1))
    kv_other = swap(kv_give)
    kv_gain = jnp.concatenate(
        [
            in_order(first, kv_mine[:, :n_kv], kv_other[:, :n_kv], 1),
            kv_mine[:, n_kv:] + kv_other[:, n_kv:],
        ],
        axis=1,
    )
    kv_gain = kv_gain + fetch(kv_gain, "t", 1)
    return (
        result,
        second_out,
        tokens_grad,
        kv_gain[:, 2 * n_kv],
        q_grad,
        kv_gain[:, : 2 * n_kv],
        out_grad_t.T,
        kv_gain[:, 2 * n_kv + 1],
        gate_grad,
        up_grad,
        down_grad_t.T,
        second_queries_grad,
    )


def solution(mesh):
    fine = Mesh(mesh.devices.reshape(2, 4, 4, 2, 2), ("x", "z", "y", "c", "t"))
    seq = ("x", "z", "y", "c")
    rows, both, turned_both = P(seq, None), P(seq, "t"), P("t", seq)
    in_specs = (
        rows, P(), P(seq), both, rows, turned_both, P(seq), both, both, turned_both, both, rows, both,
    )
    out_specs = (
        rows, both, rows, P(seq), both, rows, turned_both, P(seq), both, both, turned_both, both,
    )
    return jax.shard_map(
        on_device, mesh=fine, in_specs=in_specs, out_specs=out_specs, check_vma=False
    )
```

profile of v0, /device:TPU:1, one launch (start us, length us, event | category | flops | bytes accessed | tf_op | source)
XLA Modules:
  0.0 431.5 jit_solution(4013199851617713696)
XLA Ops:
  16.0 4.1 collective-permute-done.4
  22.5 2.9 collective-permute-start.10
  25.8 3.8 collective-permute-start.6
  30.3 2.8 collective-permute-done.11
  38.8 3.8 collective-permute-start.14
  47.6 6.6 %collective-permute-done.14.refs_5_.refs_13_.refs_6_.refs_7_.refs_15_ = bf16[256,1280]{1,0:T(8,128)(2,1)S(1)} collective-permute-done((bf16[256,1280]{1,0:T(8,128)(2,1)S(1)}, bf16[256,1280]{1,0:T(8,128)(2,1)S(1)}, u32[]{:S(2)}, u32[]{:S(2)}) %collective-permute-start.14) | collective-permute-done | bytes 655392 | tf_op jit(solution)/shard_map/ppermute | solution.py:22
  54.2 3.2 collective-permute-done.15.refs_7_.refs_15_.refs_8_.refs_9_.refs_17_
  57.5 8.2 %collective-permute-done.12.refs_1_.refs_9_.refs_2_.refs_3_.refs_11_ = bf16[256,1280]{1,0:T(8,128)(2,1)S(1)} collective-permute-done((bf16[256,1280]{1,0:T(8,128)(2,1)}, bf16[256,1280]{1,0:T(8,128)(2,1)S(1)}, u32[]{:S(2)}, u32[]{:S(2)}) %collective-permute-start.12) | collective-permute-done | bytes 655392 | tf_op jit(solution)/shard_map/ppermute | solution.py:22
  65.7 3.1 collective-permute-done.13.refs_3_.refs_11_.refs_4_.refs_5_.refs_13_
  72.1 7.7 %collective-permute-done.18 = bf16[128,1280]{1,0:T(8,128)(2,1)S(1)} collective-permute-done((bf16[128,1280]{1,0:T(8,128)(2,1)S(1)}, bf16[128,1280]{1,0:T(8,128)(2,1)S(1)}, u32[]{:S(2)}, u32[]{:S(2)}) %collective-permute-start.18) | collective-permute-done | bytes 327712 | tf_op jit(solution)/shard_map/ppermute | solution.py:22
  79.8 2.7 collective-permute-done.16
  82.6 3.7 collective-permute-done.17
  89.7 28.0 %all_to_all.15 = bf16[16,256,128]{2,1,0:T(8,128)(2,1)S(1)} all-to-all(bf16[16,256,128]{2,1,0:T(8,128)(2,1)S(1)} %broadcast_in_dim.4), channel_id=1, replica_groups=mesh['x'=2,'z'=4,'y'=4,'c'=2,'t'=2] {'z','y'}, dimensions={0} | all-to-all | bytes 2097152 | tf_op jit(solution)/shard_map/all_to_all | solution.py:826
  117.7 19.6 %collective-permute-start.20 = (bf16[4096,128]{1,0:T(8,128)(2,1)S(1)}, bf16[4096,128]{1,0:T(8,128)(2,1)S(1)}, u32[]{:S(2)}, u32[]{:S(2)}) collective-permute-start(bf16[4096,128]{1,0:T(8,128)(2,1)S(1)} %bitcast.40), channel_id=1, source_target_pairs={{2,0},{0,2},{3,1},{1,3},{6,4},{4,6},{7,5},{5,7},{10,8},{8,10},{11,... | collective-permute-start | bytes 3145736 | tf_op jit(solution)/shard_map/ppermute | solution.py:22
  144.2 7.1 %attend.1 = (f32[8,128,256]{2,1,0:T(8,128)S(1)}, f32[8,1,256]{2,1,0:T(1,128)S(1)}) custom-call(s32[4]{0:T(128)S(1)} %copy-done.41, s32[2,4]{1,0:T(2,128)S(1)} %copy-done.43, bf16[8,128,256]{2,1,0:T(8,128)(2,1)S(1)} %pad_maximum_fusion.2.qt_ref, bf16[4096,128]{1,0:T(8,128)(2,1)S(1)} %get-tuple-element.122.k_ref, bf16[128,4096]{1,0:T(8,128)(2,1)S(1)} %get-tuple-element.123.vt_ref), custom_call_target="tpu_custom_call" | custom-call | flops 1024 | bytes 1024 | tf_op jit(solution)/shard_map/attend/pallas_call | solution.py:605
  158.3 12.5 %collective-permute-done.22 = bf16[128,2048]{1,0:T(8,128)(2,1)S(1)} collective-permute-done((bf16[128,2048]{1,0:T(8,128)(2,1)S(1)}, bf16[128,2048]{1,0:T(8,128)(2,1)S(1)}, u32[]{:S(2)}, u32[]{:S(2)}) %collective-permute-start.22) | collective-permute-done | bytes 524320 | tf_op jit(solution)/shard_map/ppermute | solution.py:22
  177.7 26.2 %feed_forward.1 = (bf16[2048,4224]{1,0:T(8,128)(2,1)}, bf16[128,2048]{1,0:T(8,128)(2,1)}, bf16[128,2048]{1,0:T(8,128)(2,1)}, bf16[128,2048]{1,0:T(8,128)(2,1)}, bf16[128,2048]{1,0:T(8,128)(2,1)}) custom-call(s32[4]{0:T(128)} %pad_add_fusion.pos_ref, bf16[2048,256]{1,0:T(8,128)(2,1)} %bitcast.39, bf16[2048,256]{1,0:T(8,128)(2,1)} %bitcast.38, ...), custom_call_target="tpu_custom_call" | custom-call | flops 1024 | bytes 1024 | tf_op jit(solution)/shard_map/feed_forward/pallas_call | solution.py:327
  209.8 12.4 %collective-permute-done.25 = bf16[128,2048]{1,0:T(8,128)(2,1)S(1)} collective-permute-done((bf16[128,2048]{1,0:T(8,128)(2,1)S(1)}, bf16[128,2048]{1,0:T(8,128)(2,1)S(1)}, u32[]{:S(2)}, u32[]{:S(2)}) %collective-permute-start.25) | collective-permute-done | bytes 524320 | tf_op jit(solution)/shard_map/ppermute | solution.py:22
  231.5 7.9 %attend_back.1 = (f32[8,128,256]{2,1,0:T(8,128)S(1)}, f32[4096,128]{1,0:T(8,128)S(1)}, bf16[4096,128]{1,0:T(8,128)(2,1)S(1)}) custom-call(s32[4]{0:T(128)S(1)} %copy-done.42, s32[2,4]{1,0:T(2,128)S(1)} %copy-done.43, bf16[8,128,256]{2,1,0:T(8,128)(2,1)S(1)} %copy-done.16, bf16[8,128,256]{2,1,0:T(8,128)(2,1)S(1)} %pad_maximum_fusion.3.dot_ref, ...), custom_call_target="tpu_custom_call" | custom-call | flops 1024 | bytes 1024 | tf_op jit(solution)/shard_map/attend_back/pallas_call | solution.py:688
  241.1 3.4 weight_chunks.1
  249.2 38.8 %all-to-all-start.1 = ((bf16[16,256,128]{2,1,0:T(8,128)(2,1)}), bf16[16,256,128]{2,1,0:T(8,128)(2,1)}, u32[]{:S(2)}, u32[]{:S(2)}) async-start(bf16[16,256,128]{2,1,0:T(8,128)(2,1)} %bitcast.49), calls=%async_computation.1 | async-start | bytes 2097152 | tf_op jit(solution)/shard_map/all_to_all | solution.py:871
  290.4 23.3 %all-to-all-done.1 = bf16[16,256,128]{2,1,0:T(8,128)(2,1)} async-done(((bf16[16,256,128]{2,1,0:T(8,128)(2,1)}), bf16[16,256,128]{2,1,0:T(8,128)(2,1)}, u32[]{:S(2)}, u32[]{:S(2)}) %all-to-all-start.1) | async-done | bytes 1048608 | tf_op jit(solution)/shard_map/all_to_all | solution.py:871
  322.3 2.7 collective-permute-start.31
  333.5 6.6 %all-to-all-start.2 = ((bf16[32,2,32,256]{3,2,1,0:T(8,128)(2,1)}), bf16[32,2,32,256]{3,2,1,0:T(8,128)(2,1)}, u32[]{:S(2)}, u32[]{:S(2)}) async-start(bf16[32,2,32,256]{3,2,1,0:T(8,128)(2,1)} %bitcast.24), calls=%async_computation.2 | async-start | bytes 2097152 | tf_op jit(solution)/shard_map/all_to_all | solution.py:884
  340.1 2.7 collective-permute-start.36
  344.5 14.0 %collective-permute-done.32 = bf16[256,1024]{1,0:T(8,128)(2,1)} collective-permute-done((bf16[256,1024]{1,0:T(8,128)(2,1)S(1)}, bf16[256,1024]{1,0:T(8,128)(2,1)}, u32[]{:S(2)}, u32[]{:S(2)}) %collective-permute-start.32) | collective-permute-done | bytes 524320 | tf_op jit(solution)/shard_map/ppermute | solution.py:22
  362.0 7.0 %collective-permute-done.33 = bf16[256,1024]{1,0:T(8,128)(2,1)} collective-permute-done((bf16[256,1024]{1,0:T(8,128)(2,1)}, bf16[256,1024]{1,0:T(8,128)(2,1)}, u32[]{:S(2)}, u32[]{:S(2)}) %collective-permute-start.33) | collective-permute-done | bytes 524320 | tf_op jit(solution)/shard_map/ppermute | solution.py:22
  371.3 4.7 %all-to-all-done.2 = bf16[32,2,32,256]{3,2,1,0:T(8,128)(2,1)} async-done(((bf16[32,2,32,256]{3,2,1,0:T(8,128)(2,1)}), bf16[32,2,32,256]{3,2,1,0:T(8,128)(2,1)}, u32[]{:S(2)}, u32[]{:S(2)}) %all-to-all-start.2) | async-done | bytes 1048608 | tf_op jit(solution)/shard_map/all_to_all | solution.py:884
  377.6 4.2 collective-permute-start.40
  396.3 3.7 collective-permute-start.39
  402.6 11.0 %collective-permute-done.46 = bf16[64,4224]{1,0:T(8,128)(2,1)S(1)} collective-permute-done((bf16[64,4224]{1,0:T(8,128)(2,1)S(1)}, bf16[64,4224]{1,0:T(8,128)(2,1)S(1)}, u32[]{:S(2)}, u32[]{:S(2)}) %collective-permute-start.46) | collective-permute-done | bytes 540704 | tf_op jit(solution)/shard_map/ppermute | solution.py:22
  417.5 2.8 collective-permute-start.48
  (342 shorter events, 124.5 us)
Async XLA Ops:
  7.2 170.5 %all-gather.2.cloned.1.call-start = ((), (), s32[]{:S(2)}) async-start(), calls=%async_computation.4 | async-start | bytes 18382848 | tf_op jit(solution)/shard_map/all_gather | solution.py:797
  21.1 16.4 %collective-permute-start.5 = (bf16[64,4224]{1,0:T(8,128)(2,1)S(1)}, bf16[64,4224]{1,0:T(8,128)(2,1)S(1)}, u32[]{:S(2)}, u32[]{:S(2)}) collective-permute-start(bf16[64,4224]{1,0:T(8,128)(2,1)S(1)} %pad_maximum_fusion.1), channel_id=1, source_target_pairs={{64,0},{0,64},{65,1},{1,65},{66,2},{2,66},{67,3},{3,67},{68,4},{4,... | collective-permute-start | bytes 1622024 | tf_op jit(solution)/shard_map/ppermute | solution.py:22
  38.6 355.1 %reduce-scatter.2.cloned.1.call-start = ((), (), s32[]{:S(2)}) async-start(), calls=%async_computation.5 | async-start | bytes 18382848 | tf_op jit(solution)/shard_map/reduce_scatter | solution.py:842
  38.8 15.4 %collective-permute-start.14 = (bf16[256,1280]{1,0:T(8,128)(2,1)S(1)}, bf16[256,1280]{1,0:T(8,128)(2,1)S(1)}, u32[]{:S(2)}, u32[]{:S(2)}) collective-permute-start(bf16[256,1280]{1,0:T(8,128)(2,1)S(1)} %constant_dynamic-update-slice_fusion.4.refs_4_.refs_12_.refs_5_.refs_6_.refs_14_), channel_id=1, source_target_pairs={{16,0},{32,16},{48,32},{0,48},{17,1},{33,17},{49,33},{1,49},{18,2}... | collective-permute-start | bytes 1966088 | tf_op jit(solution)/shard_map/ppermute | solution.py:22
  42.6 14.8 %collective-permute-start.15 = (bf16[256,1280]{1,0:T(8,128)(2,1)S(1)}, bf16[256,1280]{1,0:T(8,128)(2,1)S(1)}, u32[]{:S(2)}, u32[]{:S(2)}) collective-permute-start(bf16[256,1280]{1,0:T(8,128)(2,1)S(1)} %constant_dynamic-update-slice_fusion.4.refs_4_.refs_12_.refs_5_.refs_6_.refs_14_), channel_id=1, source_target_pairs={{48,0},{0,16},{16,32},{32,48},{49,1},{1,17},{17,33},{33,49},{50,2}... | collective-permute-start | bytes 1966088 | tf_op jit(solution)/shard_map/ppermute | solution.py:22
  45.4 20.3 %collective-permute-start.12 = (bf16[256,1280]{1,0:T(8,128)(2,1)}, bf16[256,1280]{1,0:T(8,128)(2,1)S(1)}, u32[]{:S(2)}, u32[]{:S(2)}) collective-permute-start(bf16[256,1280]{1,0:T(8,128)(2,1)} %constant_dynamic-update-slice_fusion.refs_0_.refs_8_.refs_1_.refs_2_.refs_10_), channel_id=1, source_target_pairs={{4,0},{8,4},{12,8},{0,12},{5,1},{9,5},{13,9},{1,13},{6,2},{10,6},{... | collective-permute-start | bytes 1966088 | tf_op jit(solution)/shard_map/ppermute | solution.py:22
  47.3 21.4 %collective-permute-start.13 = (bf16[256,1280]{1,0:T(8,128)(2,1)}, bf16[256,1280]{1,0:T(8,128)(2,1)S(1)}, u32[]{:S(2)}, u32[]{:S(2)}) collective-permute-start(bf16[256,1280]{1,0:T(8,128)(2,1)} %constant_dynamic-update-slice_fusion.refs_0_.refs_8_.refs_1_.refs_2_.refs_10_), channel_id=1, source_target_pairs={{12,0},{0,4},{4,8},{8,12},{13,1},{1,5},{5,9},{9,13},{14,2},{2,6},{... | collective-permute-start | bytes 1966088 | tf_op jit(solution)/shard_map/ppermute | solution.py:22
  68.8 11.0 %collective-permute-start.18 = (bf16[128,1280]{1,0:T(8,128)(2,1)S(1)}, bf16[128,1280]{1,0:T(8,128)(2,1)S(1)}, u32[]{:S(2)}, u32[]{:S(2)}) collective-permute-start(bf16[128,1280]{1,0:T(8,128)(2,1)S(1)} %slice.222), channel_id=1, source_target_pairs={{16,0},{32,16},{48,32},{0,48},{17,1},{33,17},{49,33},{1,49},{18,2}... | collective-permute-start | bytes 983048 | tf_op jit(solution)/shard_map/ppermute | solution.py:22
  68.9 13.6 %collective-permute-start.16 = (bf16[128,1280]{1,0:T(8,128)(2,1)S(1)}, bf16[128,1280]{1,0:T(8,128)(2,1)S(1)}, u32[]{:S(2)}, u32[]{:S(2)}) collective-permute-start(bf16[128,1280]{1,0:T(8,128)(2,1)S(1)} %slice.220), channel_id=1, source_target_pairs={{4,0},{8,4},{12,8},{0,12},{5,1},{9,5},{13,9},{1,13},{6,2},{10,6},{... | collective-permute-start | bytes 983048 | tf_op jit(solution)/shard_map/ppermute | solution.py:22
  69.4 13.1 %collective-permute-start.19 = (bf16[128,1280]{1,0:T(8,128)(2,1)S(1)}, bf16[128,1280]{1,0:T(8,128)(2,1)S(1)}, u32[]{:S(2)}, u32[]{:S(2)}) collective-permute-start(bf16[128,1280]{1,0:T(8,128)(2,1)S(1)} %slice.223), channel_id=1, source_target_pairs={{48,0},{0,16},{16,32},{32,48},{49,1},{1,17},{17,33},{33,49},{50,2}... | collective-permute-start | bytes 983048 | tf_op jit(solution)/shard_map/ppermute | solution.py:22
  70.9 15.4 %collective-permute-start.17 = (bf16[128,1280]{1,0:T(8,128)(2,1)S(1)}, bf16[128,1280]{1,0:T(8,128)(2,1)S(1)}, u32[]{:S(2)}, u32[]{:S(2)}) collective-permute-start(bf16[128,1280]{1,0:T(8,128)(2,1)S(1)} %slice.221), channel_id=1, source_target_pairs={{12,0},{0,4},{4,8},{8,12},{13,1},{1,5},{5,9},{9,13},{14,2},{2,6},{... | collective-permute-start | bytes 983048 | tf_op jit(solution)/shard_map/ppermute | solution.py:22
  117.7 22.7 %collective-permute-start.20 = (bf16[4096,128]{1,0:T(8,128)(2,1)S(1)}, bf16[4096,128]{1,0:T(8,128)(2,1)S(1)}, u32[]{:S(2)}, u32[]{:S(2)}) collective-permute-start(bf16[4096,128]{1,0:T(8,128)(2,1)S(1)} %bitcast.40), channel_id=1, source_target_pairs={{2,0},{0,2},{3,1},{1,3},{6,4},{4,6},{7,5},{5,7},{10,8},{8,10},{11,... | collective-permute-start | bytes 3145736 | tf_op jit(solution)/shard_map/ppermute | solution.py:22
  155.9 15.0 %collective-permute-start.22 = (bf16[128,2048]{1,0:T(8,128)(2,1)S(1)}, bf16[128,2048]{1,0:T(8,128)(2,1)S(1)}, u32[]{:S(2)}, u32[]{:S(2)}) collective-permute-start(bf16[128,2048]{1,0:T(8,128)(2,1)S(1)} %add_convert_fusion.4), channel_id=1, source_target_pairs={{1,0},{0,1},{3,2},{2,3},{5,4},{4,5},{7,6},{6,7},{9,8},{8,9},{11,10... | collective-permute-start | bytes 1572872 | tf_op jit(solution)/shard_map/ppermute | solution.py:22
  207.5 14.7 %collective-permute-start.25 = (bf16[128,2048]{1,0:T(8,128)(2,1)S(1)}, bf16[128,2048]{1,0:T(8,128)(2,1)S(1)}, u32[]{:S(2)}, u32[]{:S(2)}) collective-permute-start(bf16[128,2048]{1,0:T(8,128)(2,1)S(1)} %add_convert_fusion.3), channel_id=1, source_target_pairs={{1,0},{0,1},{3,2},{2,3},{5,4},{4,5},{7,6},{6,7},{9,8},{8,9},{11,10... | collective-permute-start | bytes 1572872 | tf_op jit(solution)/shard_map/ppermute | solution.py:22
  245.7 42.3 %collective-permute-start.29 = (bf16[128,2048]{1,0:T(8,128)(2,1)}, bf16[128,2048]{1,0:T(8,128)(2,1)}, u32[]{:S(2)}, u32[]{:S(2)}) collective-permute-start(bf16[128,2048]{1,0:T(8,128)(2,1)} %add_convert_fusion.2), channel_id=1, source_target_pairs={{1,0},{0,1},{3,2},{2,3},{5,4},{4,5},{7,6},{6,7},{9,8},{8,9},{11,10... | collective-permute-start | bytes 1572872 | tf_op jit(solution)/shard_map/ppermute | solution.py:22
  249.2 64.4 %all-to-all-start.1 = ((bf16[16,256,128]{2,1,0:T(8,128)(2,1)}), bf16[16,256,128]{2,1,0:T(8,128)(2,1)}, u32[]{:S(2)}, u32[]{:S(2)}) async-start(bf16[16,256,128]{2,1,0:T(8,128)(2,1)} %bitcast.49), calls=%async_computation.1 | async-start | bytes 2097152 | tf_op jit(solution)/shard_map/all_to_all | solution.py:871
  322.3 17.8 %collective-permute-start.31 = (bf16[128,2048]{1,0:T(8,128)(2,1)}, bf16[128,2048]{1,0:T(8,128)(2,1)}, u32[]{:S(2)}, u32[]{:S(2)}) collective-permute-start(bf16[128,2048]{1,0:T(8,128)(2,1)} %add_convert_fusion.1), channel_id=1, source_target_pairs={{1,0},{0,1},{3,2},{2,3},{5,4},{4,5},{7,6},{6,7},{9,8},{8,9},{11,10... | collective-permute-start | bytes 1572872 | tf_op jit(solution)/shard_map/ppermute | solution.py:22
  327.1 31.4 %collective-permute-start.32 = (bf16[256,1024]{1,0:T(8,128)(2,1)S(1)}, bf16[256,1024]{1,0:T(8,128)(2,1)}, u32[]{:S(2)}, u32[]{:S(2)}) collective-permute-start(bf16[256,1024]{1,0:T(8,128)(2,1)S(1)} %copy-done.55), channel_id=1, source_target_pairs={{12,0},{0,4},{4,8},{8,12},{13,1},{1,5},{5,9},{9,13},{14,2},{2,6},{... | collective-permute-start | bytes 1572872 | tf_op jit(solution)/shard_map/ppermute | solution.py:22
  327.4 41.7 %collective-permute-start.33 = (bf16[256,1024]{1,0:T(8,128)(2,1)}, bf16[256,1024]{1,0:T(8,128)(2,1)}, u32[]{:S(2)}, u32[]{:S(2)}) collective-permute-start(bf16[256,1024]{1,0:T(8,128)(2,1)} %get-tuple-element.159), channel_id=1, source_target_pairs={{8,0},{12,4},{0,8},{4,12},{9,1},{13,5},{1,9},{5,13},{10,2},{14,6},... | collective-permute-start | bytes 1572872 | tf_op jit(solution)/shard_map/ppermute | solution.py:22
  327.4 41.7 %collective-permute-start.34 = (bf16[256,1024]{1,0:T(8,128)(2,1)S(1)}, bf16[256,1024]{1,0:T(8,128)(2,1)}, u32[]{:S(2)}, u32[]{:S(2)}) collective-permute-start(bf16[256,1024]{1,0:T(8,128)(2,1)S(1)} %copy-done.53), channel_id=1, source_target_pairs={{4,0},{8,4},{12,8},{0,12},{5,1},{9,5},{13,9},{1,13},{6,2},{10,6},{... | collective-permute-start | bytes 1572872 | tf_op jit(solution)/shard_map/ppermute | solution.py:22
  329.8 39.3 %collective-permute-start.35 = (bf16[256,1024]{1,0:T(8,128)(2,1)S(1)}, bf16[256,1024]{1,0:T(8,128)(2,1)}, u32[]{:S(2)}, u32[]{:S(2)}) collective-permute-start(bf16[256,1024]{1,0:T(8,128)(2,1)S(1)} %copy-done.51), channel_id=1, source_target_pairs={{48,0},{0,16},{16,32},{32,48},{49,1},{1,17},{17,33},{33,49},{50,2}... | collective-permute-start | bytes 1572872 | tf_op jit(solution)/shard_map/ppermute | solution.py:22
  333.5 42.5 %all-to-all-start.2 = ((bf16[32,2,32,256]{3,2,1,0:T(8,128)(2,1)}), bf16[32,2,32,256]{3,2,1,0:T(8,128)(2,1)}, u32[]{:S(2)}, u32[]{:S(2)}) async-start(bf16[32,2,32,256]{3,2,1,0:T(8,128)(2,1)} %bitcast.24), calls=%async_computation.2 | async-start | bytes 2097152 | tf_op jit(solution)/shard_map/all_to_all | solution.py:884
  340.1 30.4 %collective-permute-start.36 = (bf16[256,1024]{1,0:T(8,128)(2,1)S(1)}, bf16[256,1024]{1,0:T(8,128)(2,1)S(1)}, u32[]{:S(2)}, u32[]{:S(2)}) collective-permute-start(bf16[256,1024]{1,0:T(8,128)(2,1)S(1)} %copy-done.49), channel_id=1, source_target_pairs={{32,0},{48,16},{0,32},{16,48},{33,1},{49,17},{1,33},{17,49},{34,2}... | collective-permute-start | bytes 1572872 | tf_op jit(solution)/shard_map/ppermute | solution.py:22
  358.5 12.8 %collective-permute-start.37 = (bf16[256,1024]{1,0:T(8,128)(2,1)S(1)}, bf16[256,1024]{1,0:T(8,128)(2,1)}, u32[]{:S(2)}, u32[]{:S(2)}) collective-permute-start(bf16[256,1024]{1,0:T(8,128)(2,1)S(1)} %copy-done.47), channel_id=1, source_target_pairs={{16,0},{32,16},{48,32},{0,48},{17,1},{33,17},{49,33},{1,49},{18,2}... | collective-permute-start | bytes 1572872 | tf_op jit(solution)/shard_map/ppermute | solution.py:22
  377.6 17.3 %collective-permute-start.40 = (bf16[64,1024]{1,0:T(8,128)(2,1)S(1)}, bf16[64,1024]{1,0:T(8,128)(2,1)S(1)}, u32[]{:S(2)}, u32[]{:S(2)}) collective-permute-start(bf16[64,1024]{1,0:T(8,128)(2,1)S(1)} %get-tuple-element.192), channel_id=1, source_target_pairs={{48,0},{0,16},{16,32},{32,48},{49,1},{1,17},{17,33},{33,49},{50,2}... | collective-permute-start | bytes 393224 | tf_op jit(solution)/shard_map/ppermute | solution.py:22
  381.8 14.6 %collective-permute-start.41 = (bf16[64,1024]{1,0:T(8,128)(2,1)S(1)}, bf16[64,1024]{1,0:T(8,128)(2,1)S(1)}, u32[]{:S(2)}, u32[]{:S(2)}) collective-permute-start(bf16[64,1024]{1,0:T(8,128)(2,1)S(1)} %get-tuple-element.194), channel_id=1, source_target_pairs={{32,0},{48,16},{0,32},{16,48},{33,1},{49,17},{1,33},{17,49},{34,2}... | collective-permute-start | bytes 393224 | tf_op jit(solution)/shard_map/ppermute | solution.py:22
  381.8 18.3 %collective-permute-start.42 = (bf16[64,1024]{1,0:T(8,128)(2,1)S(1)}, bf16[64,1024]{1,0:T(8,128)(2,1)S(1)}, u32[]{:S(2)}, u32[]{:S(2)}) collective-permute-start(bf16[64,1024]{1,0:T(8,128)(2,1)S(1)} %get-tuple-element.193), channel_id=1, source_target_pairs={{16,0},{32,16},{48,32},{0,48},{17,1},{33,17},{49,33},{1,49},{18,2}... | collective-permute-start | bytes 393224 | tf_op jit(solution)/shard_map/ppermute | solution.py:22
  389.8 11.5 %collective-permute-start.43 = (bf16[64,1024]{1,0:T(8,128)(2,1)}, bf16[64,1024]{1,0:T(8,128)(2,1)}, u32[]{:S(2)}, u32[]{:S(2)}) collective-permute-start(bf16[64,1024]{1,0:T(8,128)(2,1)} %get-tuple-element.195), channel_id=1, source_target_pairs={{12,0},{0,4},{4,8},{8,12},{13,1},{1,5},{5,9},{9,13},{14,2},{2,6},{... | collective-permute-start | bytes 393224 | tf_op jit(solution)/shard_map/ppermute | solution.py:22
  391.9 9.3 %collective-permute-start.44 = (bf16[64,1024]{1,0:T(8,128)(2,1)}, bf16[64,1024]{1,0:T(8,128)(2,1)}, u32[]{:S(2)}, u32[]{:S(2)}) collective-permute-start(bf16[64,1024]{1,0:T(8,128)(2,1)} %get-tuple-element.197), channel_id=1, source_target_pairs={{8,0},{12,4},{0,8},{4,12},{9,1},{13,5},{1,9},{5,13},{10,2},{14,6},... | collective-permute-start | bytes 393224 | tf_op jit(solution)/shard_map/ppermute | solution.py:22
  396.3 24.0 %collective-permute-start.39 = (f32[32,384]{1,0:T(8,128)}, f32[32,384]{1,0:T(8,128)S(1)}, u32[]{:S(2)}, u32[]{:S(2)}) collective-permute-start(f32[32,384]{1,0:T(8,128)} %pad_maximum_fusion.9), channel_id=1, source_target_pairs={{1,0},{0,1},{3,2},{2,3},{5,4},{4,5},{7,6},{6,7},{9,8},{8,9},{11,10... | collective-permute-start | bytes 147464 | tf_op jit(solution)/shard_map/ppermute | solution.py:22
  400.0 13.6 %collective-permute-start.46 = (bf16[64,4224]{1,0:T(8,128)(2,1)S(1)}, bf16[64,4224]{1,0:T(8,128)(2,1)S(1)}, u32[]{:S(2)}, u32[]{:S(2)}) collective-permute-start(bf16[64,4224]{1,0:T(8,128)(2,1)S(1)} %slice.305), channel_id=1, source_target_pairs={{64,0},{0,64},{65,1},{1,65},{66,2},{2,66},{67,3},{3,67},{68,4},{4,... | collective-permute-start | bytes 1622024 | tf_op jit(solution)/shard_map/ppermute | solution.py:22
  414.4 8.5 %collective-permute-start.49 = (f32[32,4224]{1,0:T(8,128)S(1)}, f32[32,4224]{1,0:T(8,128)S(1)}, u32[]{:S(2)}, u32[]{:S(2)}) collective-permute-start(f32[32,4224]{1,0:T(8,128)S(1)} %get-tuple-element.200), channel_id=1, source_target_pairs={{2,0},{0,2},{3,1},{1,3},{6,4},{4,6},{7,5},{5,7},{10,8},{8,10},{11,... | collective-permute-start | bytes 1622024 | tf_op jit(solution)/shard_map/ppermute | solution.py:22
  (103 other events, 942.6 us)
Sparse Core Ops, SparseCore 0:
  38.7 138.8 all-gather.1
  204.1 158.5 reduce-scatter.1
where the time goes:
time: 434 us; the launch traced here: 432 us
  waiting for transfers between devices  143 us (33%)
  starting transfers between devices  130 us (30%)
  Pallas kernels  69.7 us (16%)
  other arithmetic  32.2 us (7%)
  blocking collectives  28 us (6%)
  between operations  15.5 us (4%)
  local copies, waits for them, and re-layouts  13.8 us (3%)
    ppermute x50, waiting for transfers between devices, fetch(): return lax.ppermute(block, axis, [((i + offset) % n, i) for i in range(n)])  114 us
    ppermute x50, starting transfers between devices, fetch(): return lax.ppermute(block, axis, [((i + offset) % n, i) for i in range(n)])  84.2 us
    all_to_all x1, starting transfers between devices, on_device(): kv_parts = lax.all_to_all(kv_chip, ('z', 'y'), 0, 0)  38.8 us
    all_to_all x1, blocking collectives, on_device(): kv_all = lax.all_to_all(kv_sent, ('z', 'y'), 0, 0).reshape(-1, head_dim)  28 us
    pallas_call x1, Pallas kernels, feed_forward(): call(kernel, 'feed_forward', [SMEM_SPEC, whole, whole, tile], [tile] + [r...  26.2 us
    all_to_all x1, waiting for transfers between devices, on_device(): kv_parts = lax.all_to_all(kv_chip, ('z', 'y'), 0, 0)  23.3 us
    unnamed x170, local copies, waits for them, and re-layouts  9.65 us
  transfers between devices with their start and end apart: 54, of which 28 were waited for; matrix products, arithmetic and copies ran while one was open for 8% of the time, Pallas kernels for 10%

commit v1 on v0

--- a/solution.py
+++ b/solution.py
@@ -543,7 +543,7 @@
     return (key_place <= places) & (key_place >= starts)
 
 
-def row_places(pos_ref, docs_ref, own, rows):
+def row_places(pos_ref, docs_ref, own, rows, key_block=KEY_BLOCK):
     half = rows // 2
     base = (pos_ref[Z] * 4 + pos_ref[Y]) * rows + jnp.where(own, pos_ref[CORE] * half, 0)
     lane = lax.broadcasted_iota(jnp.int32, (1, rows), 1)
@@ -556,19 +556,21 @@
         start = start + jnp.where(base >= end, length, 0)
         starts = starts + jnp.where(places >= end, length, 0)
     last = base + jnp.where(own, half, rows) - 1
-    return places, starts, lax.div(start, KEY_BLOCK), lax.div(last, KEY_BLOCK) + 1
-
-
-def attend_kernel(pos_ref, docs_ref, qt_ref, k_ref, vt_ref, ot_ref, lse_ref, *, first_set, scale):
+    return places, starts, lax.div(start, key_block), lax.div(last, key_block) + 1
+
+
+def attend_kernel(
+    pos_ref, docs_ref, qt_ref, k_ref, vt_ref, ot_ref, lse_ref, *, first_set, scale, key_block
+):
     units, head_dim, rows = qt_ref.shape
     own = pl.program_id(0) * units >= first_set
-    places, starts, low, high = row_places(pos_ref, docs_ref, own, rows)
+    places, starts, low, high = row_places(pos_ref, docs_ref, own, rows, key_block)
 
     def step(j, carry):
-        begin = pl.multiple_of(j * KEY_BLOCK, KEY_BLOCK)
-        keys = k_ref[pl.ds(begin, KEY_BLOCK), :]
-        values = vt_ref[:, pl.ds(begin, KEY_BLOCK)]
-        allowed = allowed_keys(begin, KEY_BLOCK, places, starts)
+        begin = pl.multiple_of(j * key_block, key_block)
+        keys = k_ref[pl.ds(begin, key_block), :]
+        values = vt_ref[:, pl.ds(begin, key_block)]
+        allowed = allowed_keys(begin, key_block, places, starts)
         out = []
         for u in range(units):
             top, mass, acc = carry[u]
@@ -597,13 +599,15 @@
 
 
 def attend(pos, docs, qt, keys, values_t, scale):
-    units = 2
+    units = 1
     blocks, head_dim, rows = qt.shape
     count = keys.shape[0]
     first_set = blocks // 2
     block = pl.BlockSpec((units, head_dim, rows), lambda i, p, d: (i, 0, 0))
     return pl.pallas_call(
-        functools.partial(attend_kernel, first_set=first_set, scale=scale),
+        functools.partial(
+            attend_kernel, first_set=first_set, scale=scale, key_block=2 * KEY_BLOCK
+        ),
         grid_spec=pltpu.PrefetchScalarGridSpec(
             num_scalar_prefetch=2,
             grid=(blocks // units,),
@@ -618,7 +622,7 @@
             jax.ShapeDtypeStruct((blocks, head_dim, rows), F32),
             jax.ShapeDtypeStruct((blocks, 1, rows), F32),
         ],
-        compiler_params=pltpu.CompilerParams(vmem_limit_bytes=28 * MB),
+        compiler_params=pltpu.CompilerParams(vmem_limit_bytes=32 * MB),
         cost_estimate=SMALL,
         name="attend",
     )(pos, docs, qt, keys, values_t)
@@ -789,7 +793,7 @@
     attn_other, ffn_other, tokens_other, cot_other = tie(
         swap(attn_give), swap(ffn_give), swap(tokens), swap(out_cotangent)
     )
-    *attn_rows, ffn_mine, ffn_other = tie(*across_x(attn_mine, attn_other), ffn_mine, ffn_other)
+    attn_rows = across_x(attn_mine, attn_other)
     ffn_both = jnp.concatenate([ffn_mine, ffn_other], axis=0)
     blocks = first_blocks(attn_rows)
     ffn_got, *blocks = tie(fetch(ffn_both, "x", 1), *blocks[0], *blocks[1])
@@ -869,7 +873,11 @@
     kv_chip = (kv_mine + kv_other.astype(F32)).astype(BF).reshape(16, 2 * toks, head_dim)
     kv_chip, *attn_grads = tie(kv_chip, *attn_grads)
     kv_parts = lax.all_to_all(kv_chip, ("z", "y"), 0, 0)
-    kv_parts, ffn_sum = tie(kv_parts, ffn_sum)
+    attn_terms = scatter_first(attn_grads)
+    near = (1, 3, 5, 7)
+    kv_parts, ffn_sum, *got = tie(kv_parts, ffn_sum, *[attn_terms[i] for i in near])
+    for i, term in zip(near, got):
+        attn_terms[i] = term
     kv_sum = jnp.sum(kv_parts.astype(F32), axis=0)
     result = resid + ffn_sum
     d_keyval = jnp.where(first, rotate_rows(kv_sum, cos_r, -sin_r), kv_sum).astype(BF)
@@ -882,7 +890,7 @@
         pos, normed_t, d_keyval, tokens, d_norm_part[0], d_norm_other, ffn_gain_part[None]
     )
     kv_got = lax.all_to_all(kv_grads.reshape(32, 2, rows, -1), ("x", "z", "y"), 0, 0)
-    kv_got, *attn_terms = tie(kv_got, *scatter_first(attn_grads))
+    kv_got, *attn_terms = tie(kv_got, *attn_terms)
     ffn_got = fetch(ffn_share[64:], "x", 1)
     attn_share, attn_give, ffn_got = scatter_second(attn_terms, ffn_got)
     ffn_sums = ffn_share[:64].astype(F32) + ffn_got.astype(F32)

time: 434 us -> 420 us (0.968)
  waiting for transfers between devices: 143 us -> 132 us
  blocking collectives: 28 us -> 23.3 us
    all_to_all x1, waiting for transfers between devices: 23.3 us -> 0.01 us  [on_device(): kv_parts = lax.all_to_all(kv_chip, ('z', 'y'), 0, 0)]
    ppermute x50, waiting for transfers between devices: 114 us -> 126 us  [fetch(): return lax.ppermute(block, axis, [((i + offset) % n, i) for i in range(n)])]
    ppermute x50, starting transfers between devices: 84.2 us -> 93.4 us  [fetch(): return lax.ppermute(block, axis, [((i + offset) % n, i) for i in range(n)])]
    all_to_all x1, starting transfers between devices: 38.8 us -> 30.5 us  [on_device(): kv_parts = lax.all_to_all(kv_chip, ('z', 'y'), 0, 0)]
    all_to_all x1, blocking collectives: 28 us -> 23.3 us  [on_device(): kv_all = lax.all_to_all(kv_sent, ('z', 'y'), 0, 0).reshape(-1, head_dim)]
    unnamed x170 -> x160, local copies, waits for them, and re-layouts: 9.65 us -> 8.9 us
  transfers between devices with their start and end apart: 54 -> 54, of which waited for: 28 -> 27; matrix products, arithmetic and copies ran while one was open for 8% -> 8% of each run, Pallas kernels for 10% -> 11%
where the time goes in v1:
time: 420 us; the launch traced here: 417 us
  waiting for transfers between devices  132 us (31%)
  starting transfers between devices  129 us (31%)
  Pallas kernels  72.8 us (17%)
  other arithmetic  30.9 us (7%)
  blocking collectives  23.3 us (6%)
  between operations  15.5 us (4%)
  local copies, waits for them, and re-layouts  13.1 us (3%)
    ppermute x50, waiting for transfers between devices, fetch(): return lax.ppermute(block, axis, [((i + offset) % n, i) for i in range(n)])  126 us
    ppermute x50, starting transfers between devices, fetch(): return lax.ppermute(block, axis, [((i + offset) % n, i) for i in range(n)])  93.4 us
    all_to_all x1, starting transfers between devices, on_device(): kv_parts = lax.all_to_all(kv_chip, ('z', 'y'), 0, 0)  30.5 us
    pallas_call x1, Pallas kernels, feed_forward(): call(kernel, 'feed_forward', [SMEM_SPEC, whole, whole, tile], [tile] + [r...  26.3 us
    all_to_all x1, blocking collectives, on_device(): kv_all = lax.all_to_all(kv_sent, ('z', 'y'), 0, 0).reshape(-1, head_dim)  23.3 us
    pallas_call x1, Pallas kernels, attend(): pl.pallas_call(functools.partial(attend_kernel, first_set=first_set, scal...  10.7 us
    unnamed x160, local copies, waits for them, and re-layouts  8.9 us
  transfers between devices with their start and end apart: 54, of which 27 were waited for; matrix products, arithmetic and copies ran while one was open for 8% of the time, Pallas kernels for 11%

profile of v1, /device:TPU:1, one launch (start us, length us, event | category | flops | bytes accessed | tf_op | source)
XLA Modules:
  0.0 416.8 jit_solution(15860309288238740616)
XLA Ops:
  17.2 2.9 collective-permute-done.5
  20.1 3.1 collective-permute-start.10
  25.9 3.8 collective-permute-start.6
  35.4 2.6 collective-permute-done.8
  39.3 2.7 collective-permute-start.14
  46.5 7.1 %collective-permute-done.14.refs_5_.refs_13_.refs_6_.refs_7_.refs_15_ = bf16[256,1280]{1,0:T(8,128)(2,1)S(1)} collective-permute-done((bf16[256,1280]{1,0:T(8,128)(2,1)S(1)}, bf16[256,1280]{1,0:T(8,128)(2,1)S(1)}, u32[]{:S(2)}, u32[]{:S(2)}) %collective-permute-start.14) | collective-permute-done | bytes 655392 | tf_op jit(solution)/shard_map/ppermute | solution.py:22
  53.6 3.2 collective-permute-done.15.refs_7_.refs_15_.refs_8_.refs_9_.refs_17_
  56.8 3.9 collective-permute-done.12.refs_1_.refs_9_.refs_2_.refs_3_.refs_11_
  61.1 3.1 collective-permute-start.18
  66.8 8.4 %collective-permute-done.18 = bf16[128,1280]{1,0:T(8,128)(2,1)S(1)} collective-permute-done((bf16[128,1280]{1,0:T(8,128)(2,1)S(1)}, bf16[128,1280]{1,0:T(8,128)(2,1)S(1)}, u32[]{:S(2)}, u32[]{:S(2)}) %collective-permute-start.18) | collective-permute-done | bytes 327712 | tf_op jit(solution)/shard_map/ppermute | solution.py:22
  75.3 4.6 %collective-permute-done.16 = bf16[128,1280]{1,0:T(8,128)(2,1)S(1)} collective-permute-done((bf16[128,1280]{1,0:T(8,128)(2,1)S(1)}, bf16[128,1280]{1,0:T(8,128)(2,1)S(1)}, u32[]{:S(2)}, u32[]{:S(2)}) %collective-permute-start.16) | collective-permute-done | bytes 327712 | tf_op jit(solution)/shard_map/ppermute | solution.py:22
  85.5 23.3 %all_to_all.15 = bf16[16,256,128]{2,1,0:T(8,128)(2,1)S(1)} all-to-all(bf16[16,256,128]{2,1,0:T(8,128)(2,1)S(1)} %broadcast_in_dim.4), channel_id=1, replica_groups=mesh['x'=2,'z'=4,'y'=4,'c'=2,'t'=2] {'z','y'}, dimensions={0} | all-to-all | bytes 2097152 | tf_op jit(solution)/shard_map/all_to_all | solution.py:830
  108.8 25.8 %collective-permute-start.20 = (bf16[4096,128]{1,0:T(8,128)(2,1)S(1)}, bf16[4096,128]{1,0:T(8,128)(2,1)S(1)}, u32[]{:S(2)}, u32[]{:S(2)}) collective-permute-start(bf16[4096,128]{1,0:T(8,128)(2,1)S(1)} %bitcast.40), channel_id=1, source_target_pairs={{2,0},{0,2},{3,1},{1,3},{6,4},{4,6},{7,5},{5,7},{10,8},{8,10},{11,... | collective-permute-start | bytes 3145736 | tf_op jit(solution)/shard_map/ppermute | solution.py:22
  141.4 10.7 %attend.1 = (f32[8,128,256]{2,1,0:T(8,128)S(1)}, f32[8,1,256]{2,1,0:T(1,128)S(1)}) custom-call(s32[4]{0:T(128)S(1)} %copy-done.41, s32[2,4]{1,0:T(2,128)S(1)} %copy-done.43, bf16[8,128,256]{2,1,0:T(8,128)(2,1)S(1)} %pad_maximum_fusion.2.qt_ref, bf16[4096,128]{1,0:T(8,128)(2,1)S(1)} %get-tuple-element.118.k_ref, bf16[128,4096]{1,0:T(8,128)(2,1)S(1)} %get-tuple-element.119.vt_ref), custom_call_target="tpu_custom_call" | custom-call | flops 1024 | bytes 1024 | tf_op jit(solution)/shard_map/attend/pallas_call | solution.py:607
  156.6 3.0 collective-permute-start.22
  160.2 11.4 %collective-permute-done.22 = bf16[128,2048]{1,0:T(8,128)(2,1)S(1)} collective-permute-done((bf16[128,2048]{1,0:T(8,128)(2,1)S(1)}, bf16[128,2048]{1,0:T(8,128)(2,1)S(1)}, u32[]{:S(2)}, u32[]{:S(2)}) %collective-permute-start.22) | collective-permute-done | bytes 524320 | tf_op jit(solution)/shard_map/ppermute | solution.py:22
  177.9 26.3 %feed_forward.1 = (bf16[2048,4224]{1,0:T(8,128)(2,1)}, bf16[128,2048]{1,0:T(8,128)(2,1)}, bf16[128,2048]{1,0:T(8,128)(2,1)}, bf16[128,2048]{1,0:T(8,128)(2,1)}, bf16[128,2048]{1,0:T(8,128)(2,1)}) custom-call(s32[4]{0:T(128)} %pad_add_fusion.pos_ref, bf16[2048,256]{1,0:T(8,128)(2,1)} %bitcast.39, bf16[2048,256]{1,0:T(8,128)(2,1)} %bitcast.38, ...), custom_call_target="tpu_custom_call" | custom-call | flops 1024 | bytes 1024 | tf_op jit(solution)/shard_map/feed_forward/pallas_call | solution.py:327
  207.6 3.0 collective-permute-start.25
  210.6 11.8 %collective-permute-done.25 = bf16[128,2048]{1,0:T(8,128)(2,1)S(1)} collective-permute-done((bf16[128,2048]{1,0:T(8,128)(2,1)S(1)}, bf16[128,2048]{1,0:T(8,128)(2,1)S(1)}, u32[]{:S(2)}, u32[]{:S(2)}) %collective-permute-start.25) | collective-permute-done | bytes 524320 | tf_op jit(solution)/shard_map/ppermute | solution.py:22
  231.7 7.9 %attend_back.1 = (f32[8,128,256]{2,1,0:T(8,128)S(1)}, f32[4096,128]{1,0:T(8,128)S(1)}, bf16[4096,128]{1,0:T(8,128)(2,1)S(1)}) custom-call(s32[4]{0:T(128)S(1)} %copy-done.42, s32[2,4]{1,0:T(2,128)S(1)} %copy-done.43, bf16[8,128,256]{2,1,0:T(8,128)(2,1)S(1)} %copy-done.16, bf16[8,128,256]{2,1,0:T(8,128)(2,1)S(1)} %pad_maximum_fusion.3.dot_ref, ...), custom_call_target="tpu_custom_call" | custom-call | flops 1024 | bytes 1024 | tf_op jit(solution)/shard_map/attend_back/pallas_call | solution.py:692
  241.3 3.0 weight_chunks.1
  245.5 3.1 collective-permute-start.29
  249.8 30.5 %all-to-all-start.1 = ((bf16[16,256,128]{2,1,0:T(8,128)(2,1)}), bf16[16,256,128]{2,1,0:T(8,128)(2,1)}, u32[]{:S(2)}, u32[]{:S(2)}) async-start(bf16[16,256,128]{2,1,0:T(8,128)(2,1)} %bitcast.49), calls=%async_computation.1 | async-start | bytes 2097152 | tf_op jit(solution)/shard_map/all_to_all | solution.py:875
  288.0 27.9 %collective-permute-done.30 = bf16[256,1024]{1,0:T(8,128)(2,1)} collective-permute-done((bf16[256,1024]{1,0:T(8,128)(2,1)}, bf16[256,1024]{1,0:T(8,128)(2,1)}, u32[]{:S(2)}, u32[]{:S(2)}) %collective-permute-start.30) | collective-permute-done | bytes 524320 | tf_op jit(solution)/shard_map/ppermute | solution.py:22
  324.7 2.9 collective-permute-start.35
  336.7 4.8 %all-to-all-start.2 = ((bf16[32,2,32,256]{3,2,1,0:T(8,128)(2,1)}), bf16[32,2,32,256]{3,2,1,0:T(8,128)(2,1)}, u32[]{:S(2)}, u32[]{:S(2)}) async-start(bf16[32,2,32,256]{3,2,1,0:T(8,128)(2,1)} %bitcast.24), calls=%async_computation.2 | async-start | bytes 2097152 | tf_op jit(solution)/shard_map/all_to_all | solution.py:892
  343.2 2.6 fusion.2
  345.9 15.0 %collective-permute-done.36 = bf16[256,1024]{1,0:T(8,128)(2,1)} collective-permute-done((bf16[256,1024]{1,0:T(8,128)(2,1)S(1)}, bf16[256,1024]{1,0:T(8,128)(2,1)}, u32[]{:S(2)}, u32[]{:S(2)}) %collective-permute-start.36) | collective-permute-done | bytes 524320 | tf_op jit(solution)/shard_map/ppermute | solution.py:22
  361.8 5.9 %all-to-all-done.2 = bf16[32,2,32,256]{3,2,1,0:T(8,128)(2,1)} async-done(((bf16[32,2,32,256]{3,2,1,0:T(8,128)(2,1)}), bf16[32,2,32,256]{3,2,1,0:T(8,128)(2,1)}, u32[]{:S(2)}, u32[]{:S(2)}) %all-to-all-start.2) | async-done | bytes 1048608 | tf_op jit(solution)/shard_map/all_to_all | solution.py:892
  382.7 2.7 collective-permute-start.39
  388.9 10.2 %collective-permute-done.46 = bf16[64,4224]{1,0:T(8,128)(2,1)S(1)} collective-permute-done((bf16[64,4224]{1,0:T(8,128)(2,1)S(1)}, bf16[64,4224]{1,0:T(8,128)(2,1)S(1)}, u32[]{:S(2)}, u32[]{:S(2)}) %collective-permute-start.46) | collective-permute-done | bytes 540704 | tf_op jit(solution)/shard_map/ppermute | solution.py:22
  403.0 2.6 collective-permute-start.48
  (333 shorter events, 121.6 us)
Async XLA Ops:
  7.2 170.8 %all-gather.2.cloned.1.call-start = ((), (), s32[]{:S(2)}) async-start(), calls=%async_computation.4 | async-start | bytes 18382848 | tf_op jit(solution)/shard_map/all_gather | solution.py:801
  17.0 21.0 %collective-permute-start.4 = (bf16[64,4224]{1,0:T(8,128)(2,1)S(1)}, bf16[64,4224]{1,0:T(8,128)(2,1)S(1)}, u32[]{:S(2)}, u32[]{:S(2)}) collective-permute-start(bf16[64,4224]{1,0:T(8,128)(2,1)S(1)} %pad_maximum_fusion.1), channel_id=1, source_target_pairs={{64,0},{0,64},{65,1},{1,65},{66,2},{2,66},{67,3},{3,67},{68,4},{4,... | collective-permute-start | bytes 1622024 | tf_op jit(solution)/shard_map/ppermute | solution.py:22
  20.1 9.6 %collective-permute-start.10 = (bf16[64,1280]{1,0:T(8,128)(2,1)S(1)}, bf16[64,1280]{1,0:T(8,128)(2,1)S(1)}, u32[]{:S(2)}, u32[]{:S(2)}) collective-permute-start(bf16[64,1280]{1,0:T(8,128)(2,1)S(1)} %pad_maximum_fusion.7), channel_id=1, source_target_pairs={{8,0},{12,4},{0,8},{4,12},{9,1},{13,5},{1,9},{5,13},{10,2},{14,6},... | collective-permute-start | bytes 491528 | tf_op jit(solution)/shard_map/ppermute | solution.py:22
  23.6 9.0 %collective-permute-start.9 = (bf16[64,1280]{1,0:T(8,128)(2,1)S(1)}, bf16[64,1280]{1,0:T(8,128)(2,1)S(1)}, u32[]{:S(2)}, u32[]{:S(2)}) collective-permute-start(bf16[64,1280]{1,0:T(8,128)(2,1)S(1)} %pad_maximum_fusion.7), channel_id=1, source_target_pairs={{4,0},{8,4},{12,8},{0,12},{5,1},{9,5},{13,9},{1,13},{6,2},{10,6},{... | collective-permute-start | bytes 491528 | tf_op jit(solution)/shard_map/ppermute | solution.py:22
  39.1 341.2 %reduce-scatter.2.cloned.1.call-start = ((), (), s32[]{:S(2)}) async-start(), calls=%async_computation.5 | async-start | bytes 18382848 | tf_op jit(solution)/shard_map/reduce_scatter | solution.py:846
  39.3 14.3 %collective-permute-start.14 = (bf16[256,1280]{1,0:T(8,128)(2,1)S(1)}, bf16[256,1280]{1,0:T(8,128)(2,1)S(1)}, u32[]{:S(2)}, u32[]{:S(2)}) collective-permute-start(bf16[256,1280]{1,0:T(8,128)(2,1)S(1)} %constant_dynamic-update-slice_fusion.4.refs_4_.refs_12_.refs_5_.refs_6_.refs_14_), channel_id=1, source_target_pairs={{16,0},{32,16},{48,32},{0,48},{17,1},{33,17},{49,33},{1,49},{18,2}... | collective-permute-start | bytes 1966088 | tf_op jit(solution)/shard_map/ppermute | solution.py:22
  42.0 14.8 %collective-permute-start.15 = (bf16[256,1280]{1,0:T(8,128)(2,1)S(1)}, bf16[256,1280]{1,0:T(8,128)(2,1)S(1)}, u32[]{:S(2)}, u32[]{:S(2)}) collective-permute-start(bf16[256,1280]{1,0:T(8,128)(2,1)S(1)} %constant_dynamic-update-slice_fusion.4.refs_4_.refs_12_.refs_5_.refs_6_.refs_14_), channel_id=1, source_target_pairs={{48,0},{0,16},{16,32},{32,48},{49,1},{1,17},{17,33},{33,49},{50,2}... | collective-permute-start | bytes 1966088 | tf_op jit(solution)/shard_map/ppermute | solution.py:22
  44.7 16.0 %collective-permute-start.12 = (bf16[256,1280]{1,0:T(8,128)(2,1)}, bf16[256,1280]{1,0:T(8,128)(2,1)S(1)}, u32[]{:S(2)}, u32[]{:S(2)}) collective-permute-start(bf16[256,1280]{1,0:T(8,128)(2,1)} %constant_dynamic-update-slice_fusion.refs_0_.refs_8_.refs_1_.refs_2_.refs_10_), channel_id=1, source_target_pairs={{4,0},{8,4},{12,8},{0,12},{5,1},{9,5},{13,9},{1,13},{6,2},{10,6},{... | collective-permute-start | bytes 1966088 | tf_op jit(solution)/shard_map/ppermute | solution.py:22
  44.7 16.4 %collective-permute-start.13 = (bf16[256,1280]{1,0:T(8,128)(2,1)}, bf16[256,1280]{1,0:T(8,128)(2,1)S(1)}, u32[]{:S(2)}, u32[]{:S(2)}) collective-permute-start(bf16[256,1280]{1,0:T(8,128)(2,1)} %constant_dynamic-update-slice_fusion.refs_0_.refs_8_.refs_1_.refs_2_.refs_10_), channel_id=1, source_target_pairs={{12,0},{0,4},{4,8},{8,12},{13,1},{1,5},{5,9},{9,13},{14,2},{2,6},{... | collective-permute-start | bytes 1966088 | tf_op jit(solution)/shard_map/ppermute | solution.py:22
  61.1 14.1 %collective-permute-start.18 = (bf16[128,1280]{1,0:T(8,128)(2,1)S(1)}, bf16[128,1280]{1,0:T(8,128)(2,1)S(1)}, u32[]{:S(2)}, u32[]{:S(2)}) collective-permute-start(bf16[128,1280]{1,0:T(8,128)(2,1)S(1)} %slice.222), channel_id=1, source_target_pairs={{16,0},{32,16},{48,32},{0,48},{17,1},{33,17},{49,33},{1,49},{18,2}... | collective-permute-start | bytes 983048 | tf_op jit(solution)/shard_map/ppermute | solution.py:22
  64.3 15.6 %collective-permute-start.16 = (bf16[128,1280]{1,0:T(8,128)(2,1)S(1)}, bf16[128,1280]{1,0:T(8,128)(2,1)S(1)}, u32[]{:S(2)}, u32[]{:S(2)}) collective-permute-start(bf16[128,1280]{1,0:T(8,128)(2,1)S(1)} %slice.220), channel_id=1, source_target_pairs={{4,0},{8,4},{12,8},{0,12},{5,1},{9,5},{13,9},{1,13},{6,2},{10,6},{... | collective-permute-start | bytes 983048 | tf_op jit(solution)/shard_map/ppermute | solution.py:22
  65.5 14.4 %collective-permute-start.19 = (bf16[128,1280]{1,0:T(8,128)(2,1)S(1)}, bf16[128,1280]{1,0:T(8,128)(2,1)S(1)}, u32[]{:S(2)}, u32[]{:S(2)}) collective-permute-start(bf16[128,1280]{1,0:T(8,128)(2,1)S(1)} %slice.223), channel_id=1, source_target_pairs={{48,0},{0,16},{16,32},{32,48},{49,1},{1,17},{17,33},{33,49},{50,2}... | collective-permute-start | bytes 983048 | tf_op jit(solution)/shard_map/ppermute | solution.py:22
  65.6 16.5 %collective-permute-start.17 = (bf16[128,1280]{1,0:T(8,128)(2,1)S(1)}, bf16[128,1280]{1,0:T(8,128)(2,1)S(1)}, u32[]{:S(2)}, u32[]{:S(2)}) collective-permute-start(bf16[128,1280]{1,0:T(8,128)(2,1)S(1)} %slice.221), channel_id=1, source_target_pairs={{12,0},{0,4},{4,8},{8,12},{13,1},{1,5},{5,9},{9,13},{14,2},{2,6},{... | collective-permute-start | bytes 983048 | tf_op jit(solution)/shard_map/ppermute | solution.py:22
  108.8 28.9 %collective-permute-start.20 = (bf16[4096,128]{1,0:T(8,128)(2,1)S(1)}, bf16[4096,128]{1,0:T(8,128)(2,1)S(1)}, u32[]{:S(2)}, u32[]{:S(2)}) collective-permute-start(bf16[4096,128]{1,0:T(8,128)(2,1)S(1)} %bitcast.40), channel_id=1, source_target_pairs={{2,0},{0,2},{3,1},{1,3},{6,4},{4,6},{7,5},{5,7},{10,8},{8,10},{11,... | collective-permute-start | bytes 3145736 | tf_op jit(solution)/shard_map/ppermute | solution.py:22
  156.6 15.0 %collective-permute-start.22 = (bf16[128,2048]{1,0:T(8,128)(2,1)S(1)}, bf16[128,2048]{1,0:T(8,128)(2,1)S(1)}, u32[]{:S(2)}, u32[]{:S(2)}) collective-permute-start(bf16[128,2048]{1,0:T(8,128)(2,1)S(1)} %add_convert_fusion.4), channel_id=1, source_target_pairs={{1,0},{0,1},{3,2},{2,3},{5,4},{4,5},{7,6},{6,7},{9,8},{8,9},{11,10... | collective-permute-start | bytes 1572872 | tf_op jit(solution)/shard_map/ppermute | solution.py:22
  207.6 14.7 %collective-permute-start.25 = (bf16[128,2048]{1,0:T(8,128)(2,1)S(1)}, bf16[128,2048]{1,0:T(8,128)(2,1)S(1)}, u32[]{:S(2)}, u32[]{:S(2)}) collective-permute-start(bf16[128,2048]{1,0:T(8,128)(2,1)S(1)} %add_convert_fusion.3), channel_id=1, source_target_pairs={{1,0},{0,1},{3,2},{2,3},{5,4},{4,5},{7,6},{6,7},{9,8},{8,9},{11,10... | collective-permute-start | bytes 1572872 | tf_op jit(solution)/shard_map/ppermute | solution.py:22
  245.5 40.2 %collective-permute-start.29 = (bf16[128,2048]{1,0:T(8,128)(2,1)}, bf16[128,2048]{1,0:T(8,128)(2,1)}, u32[]{:S(2)}, u32[]{:S(2)}) collective-permute-start(bf16[128,2048]{1,0:T(8,128)(2,1)} %add_convert_fusion.2), channel_id=1, source_target_pairs={{1,0},{0,1},{3,2},{2,3},{5,4},{4,5},{7,6},{6,7},{9,8},{8,9},{11,10... | collective-permute-start | bytes 1572872 | tf_op jit(solution)/shard_map/ppermute | solution.py:22
  249.8 66.2 %all-to-all-start.1 = ((bf16[16,256,128]{2,1,0:T(8,128)(2,1)}), bf16[16,256,128]{2,1,0:T(8,128)(2,1)}, u32[]{:S(2)}, u32[]{:S(2)}) async-start(bf16[16,256,128]{2,1,0:T(8,128)(2,1)} %bitcast.49), calls=%async_computation.1 | async-start | bytes 2097152 | tf_op jit(solution)/shard_map/all_to_all | solution.py:875
  280.3 35.6 %collective-permute-start.30 = (bf16[256,1024]{1,0:T(8,128)(2,1)}, bf16[256,1024]{1,0:T(8,128)(2,1)}, u32[]{:S(2)}, u32[]{:S(2)}) collective-permute-start(bf16[256,1024]{1,0:T(8,128)(2,1)} %copy-done.53), channel_id=1, source_target_pairs={{12,0},{0,4},{4,8},{8,12},{13,1},{1,5},{5,9},{9,13},{14,2},{2,6},{... | collective-permute-start | bytes 1572872 | tf_op jit(solution)/shard_map/ppermute | solution.py:22
  281.6 34.3 %collective-permute-start.31 = (bf16[256,1024]{1,0:T(8,128)(2,1)}, bf16[256,1024]{1,0:T(8,128)(2,1)}, u32[]{:S(2)}, u32[]{:S(2)}) collective-permute-start(bf16[256,1024]{1,0:T(8,128)(2,1)} %copy-done.52), channel_id=1, source_target_pairs={{4,0},{8,4},{12,8},{0,12},{5,1},{9,5},{13,9},{1,13},{6,2},{10,6},{... | collective-permute-start | bytes 1572872 | tf_op jit(solution)/shard_map/ppermute | solution.py:22
  283.0 32.9 %collective-permute-start.32 = (bf16[256,1024]{1,0:T(8,128)(2,1)}, bf16[256,1024]{1,0:T(8,128)(2,1)}, u32[]{:S(2)}, u32[]{:S(2)}) collective-permute-start(bf16[256,1024]{1,0:T(8,128)(2,1)} %copy-done.51), channel_id=1, source_target_pairs={{48,0},{0,16},{16,32},{32,48},{49,1},{1,17},{17,33},{33,49},{50,2}... | collective-permute-start | bytes 1572872 | tf_op jit(solution)/shard_map/ppermute | solution.py:22
  284.3 31.7 %collective-permute-start.33 = (bf16[256,1024]{1,0:T(8,128)(2,1)}, bf16[256,1024]{1,0:T(8,128)(2,1)}, u32[]{:S(2)}, u32[]{:S(2)}) collective-permute-start(bf16[256,1024]{1,0:T(8,128)(2,1)} %copy-done.50), channel_id=1, source_target_pairs={{16,0},{32,16},{48,32},{0,48},{17,1},{33,17},{49,33},{1,49},{18,2}... | collective-permute-start | bytes 1572872 | tf_op jit(solution)/shard_map/ppermute | solution.py:22
  324.7 16.8 %collective-permute-start.35 = (bf16[128,2048]{1,0:T(8,128)(2,1)}, bf16[128,2048]{1,0:T(8,128)(2,1)}, u32[]{:S(2)}, u32[]{:S(2)}) collective-permute-start(bf16[128,2048]{1,0:T(8,128)(2,1)} %add_convert_fusion.1), channel_id=1, source_target_pairs={{1,0},{0,1},{3,2},{2,3},{5,4},{4,5},{7,6},{6,7},{9,8},{8,9},{11,10... | collective-permute-start | bytes 1572872 | tf_op jit(solution)/shard_map/ppermute | solution.py:22
  329.6 31.3 %collective-permute-start.36 = (bf16[256,1024]{1,0:T(8,128)(2,1)S(1)}, bf16[256,1024]{1,0:T(8,128)(2,1)}, u32[]{:S(2)}, u32[]{:S(2)}) collective-permute-start(bf16[256,1024]{1,0:T(8,128)(2,1)S(1)} %copy-done.49), channel_id=1, source_target_pairs={{8,0},{12,4},{0,8},{4,12},{9,1},{13,5},{1,9},{5,13},{10,2},{14,6},... | collective-permute-start | bytes 1572872 | tf_op jit(solution)/shard_map/ppermute | solution.py:22
  332.1 29.7 %collective-permute-start.37 = (bf16[256,1024]{1,0:T(8,128)(2,1)S(1)}, bf16[256,1024]{1,0:T(8,128)(2,1)}, u32[]{:S(2)}, u32[]{:S(2)}) collective-permute-start(bf16[256,1024]{1,0:T(8,128)(2,1)S(1)} %copy-done.47), channel_id=1, source_target_pairs={{32,0},{48,16},{0,32},{16,48},{33,1},{49,17},{1,33},{17,49},{34,2}... | collective-permute-start | bytes 1572872 | tf_op jit(solution)/shard_map/ppermute | solution.py:22
  336.7 31.0 %all-to-all-start.2 = ((bf16[32,2,32,256]{3,2,1,0:T(8,128)(2,1)}), bf16[32,2,32,256]{3,2,1,0:T(8,128)(2,1)}, u32[]{:S(2)}, u32[]{:S(2)}) async-start(bf16[32,2,32,256]{3,2,1,0:T(8,128)(2,1)} %bitcast.24), calls=%async_computation.2 | async-start | bytes 2097152 | tf_op jit(solution)/shard_map/all_to_all | solution.py:892
  369.3 12.1 %collective-permute-start.40 = (bf16[64,1024]{1,0:T(8,128)(2,1)S(1)}, bf16[64,1024]{1,0:T(8,128)(2,1)S(1)}, u32[]{:S(2)}, u32[]{:S(2)}) collective-permute-start(bf16[64,1024]{1,0:T(8,128)(2,1)S(1)} %get-tuple-element.192), channel_id=1, source_target_pairs={{48,0},{0,16},{16,32},{32,48},{49,1},{1,17},{17,33},{33,49},{50,2}... | collective-permute-start | bytes 393224 | tf_op jit(solution)/shard_map/ppermute | solution.py:22
  370.6 12.1 %collective-permute-start.41 = (bf16[64,1024]{1,0:T(8,128)(2,1)S(1)}, bf16[64,1024]{1,0:T(8,128)(2,1)S(1)}, u32[]{:S(2)}, u32[]{:S(2)}) collective-permute-start(bf16[64,1024]{1,0:T(8,128)(2,1)S(1)} %get-tuple-element.194), channel_id=1, source_target_pairs={{32,0},{48,16},{0,32},{16,48},{33,1},{49,17},{1,33},{17,49},{34,2}... | collective-permute-start | bytes 393224 | tf_op jit(solution)/shard_map/ppermute | solution.py:22
  371.3 14.1 %collective-permute-start.42 = (bf16[64,1024]{1,0:T(8,128)(2,1)S(1)}, bf16[64,1024]{1,0:T(8,128)(2,1)S(1)}, u32[]{:S(2)}, u32[]{:S(2)}) collective-permute-start(bf16[64,1024]{1,0:T(8,128)(2,1)S(1)} %get-tuple-element.193), channel_id=1, source_target_pairs={{16,0},{32,16},{48,32},{0,48},{17,1},{33,17},{49,33},{1,49},{18,2}... | collective-permute-start | bytes 393224 | tf_op jit(solution)/shard_map/ppermute | solution.py:22
  378.2 9.2 %collective-permute-start.43 = (bf16[64,1024]{1,0:T(8,128)(2,1)S(1)}, bf16[64,1024]{1,0:T(8,128)(2,1)S(1)}, u32[]{:S(2)}, u32[]{:S(2)}) collective-permute-start(bf16[64,1024]{1,0:T(8,128)(2,1)S(1)} %get-tuple-element.195), channel_id=1, source_target_pairs={{12,0},{0,4},{4,8},{8,12},{13,1},{1,5},{5,9},{9,13},{14,2},{2,6},{... | collective-permute-start | bytes 393224 | tf_op jit(solution)/shard_map/ppermute | solution.py:22
  382.7 22.9 %collective-permute-start.39 = (f32[32,384]{1,0:T(8,128)S(1)}, f32[32,384]{1,0:T(8,128)S(1)}, u32[]{:S(2)}, u32[]{:S(2)}) collective-permute-start(f32[32,384]{1,0:T(8,128)S(1)} %pad_maximum_fusion.9), channel_id=1, source_target_pairs={{1,0},{0,1},{3,2},{2,3},{5,4},{4,5},{7,6},{6,7},{9,8},{8,9},{11,10... | collective-permute-start | bytes 147464 | tf_op jit(solution)/shard_map/ppermute | solution.py:22
  385.4 13.7 %collective-permute-start.46 = (bf16[64,4224]{1,0:T(8,128)(2,1)S(1)}, bf16[64,4224]{1,0:T(8,128)(2,1)S(1)}, u32[]{:S(2)}, u32[]{:S(2)}) collective-permute-start(bf16[64,4224]{1,0:T(8,128)(2,1)S(1)} %slice.305), channel_id=1, source_target_pairs={{64,0},{0,64},{65,1},{1,65},{66,2},{2,66},{67,3},{3,67},{68,4},{4,... | collective-permute-start | bytes 1622024 | tf_op jit(solution)/shard_map/ppermute | solution.py:22
  (98 other events, 949.8 us)
Sparse Core Ops, SparseCore 0:
  39.2 136.2 all-gather.1
  204.3 163.3 reduce-scatter.1

commit v2 on v1

--- a/solution.py
+++ b/solution.py
@@ -253,7 +253,7 @@
     )(pos, *[side[2] for side in sides], *operands)
 
 
-TILE = 256
+TILE = 128
 
 
 def tile_columns(hidden):

time: 420 us -> 423 us (level)
  no operation moved by 1% of the time
where the time goes in v2:
time: 423 us; the launch traced here: 419 us
  waiting for transfers between devices  133 us (31%)
  starting transfers between devices  128 us (30%)
  Pallas kernels  75.6 us (18%)
  other arithmetic  30.9 us (7%)
  blocking collectives  23.2 us (5%)
  between operations  15.5 us (4%)
  local copies, waits for them, and re-layouts  13.1 us (3%)
    ppermute x50, waiting for transfers between devices, fetch(): return lax.ppermute(block, axis, [((i + offset) % n, i) for i in range(n)])  127 us
    ppermute x50, starting transfers between devices, fetch(): return lax.ppermute(block, axis, [((i + offset) % n, i) for i in range(n)])  92.9 us
    all_to_all x1, starting transfers between devices, on_device(): kv_parts = lax.all_to_all(kv_chip, ('z', 'y'), 0, 0)  30.4 us
    pallas_call x1, Pallas kernels, feed_forward(): call(kernel, 'feed_forward', [SMEM_SPEC, whole, whole, tile], [tile] + [r...  29 us
    all_to_all x1, blocking collectives, on_device(): kv_all = lax.all_to_all(kv_sent, ('z', 'y'), 0, 0).reshape(-1, head_dim)  23.2 us
    pallas_call x1, Pallas kernels, attend(): pl.pallas_call(functools.partial(attend_kernel, first_set=first_set, scal...  10.7 us
    unnamed x160, local copies, waits for them, and re-layouts  8.9 us
  transfers between devices with their start and end apart: 54, of which 27 were waited for; matrix products, arithmetic and copies ran while one was open for 8% of the time, Pallas kernels for 11%

profile of v2, /device:TPU:1, one launch (start us, length us, event | category | flops | bytes accessed | tf_op | source)
XLA Modules:
  0.0 419.3 jit_solution(10653823267681058553)
XLA Ops:
  17.3 2.9 collective-permute-done.5
  20.2 3.1 collective-permute-start.10
  26.0 3.8 collective-permute-start.6
  35.5 2.6 collective-permute-done.8
  39.3 2.7 collective-permute-start.14
  46.5 7.1 %collective-permute-done.14.refs_5_.refs_13_.refs_6_.refs_7_.refs_15_ = bf16[256,1280]{1,0:T(8,128)(2,1)S(1)} collective-permute-done((bf16[256,1280]{1,0:T(8,128)(2,1)S(1)}, bf16[256,1280]{1,0:T(8,128)(2,1)S(1)}, u32[]{:S(2)}, u32[]{:S(2)}) %collective-permute-start.14) | collective-permute-done | bytes 655392 | tf_op jit(solution)/shard_map/ppermute | solution.py:22
  53.6 3.2 collective-permute-done.15.refs_7_.refs_15_.refs_8_.refs_9_.refs_17_
  56.8 3.9 collective-permute-done.12.refs_1_.refs_9_.refs_2_.refs_3_.refs_11_
  61.2 3.1 collective-permute-start.18
  66.8 8.4 %collective-permute-done.18 = bf16[128,1280]{1,0:T(8,128)(2,1)S(1)} collective-permute-done((bf16[128,1280]{1,0:T(8,128)(2,1)S(1)}, bf16[128,1280]{1,0:T(8,128)(2,1)S(1)}, u32[]{:S(2)}, u32[]{:S(2)}) %collective-permute-start.18) | collective-permute-done | bytes 327712 | tf_op jit(solution)/shard_map/ppermute | solution.py:22
  75.3 4.6 %collective-permute-done.16 = bf16[128,1280]{1,0:T(8,128)(2,1)S(1)} collective-permute-done((bf16[128,1280]{1,0:T(8,128)(2,1)S(1)}, bf16[128,1280]{1,0:T(8,128)(2,1)S(1)}, u32[]{:S(2)}, u32[]{:S(2)}) %collective-permute-start.16) | collective-permute-done | bytes 327712 | tf_op jit(solution)/shard_map/ppermute | solution.py:22
  85.5 23.2 %all_to_all.15 = bf16[16,256,128]{2,1,0:T(8,128)(2,1)S(1)} all-to-all(bf16[16,256,128]{2,1,0:T(8,128)(2,1)S(1)} %broadcast_in_dim.4), channel_id=1, replica_groups=mesh['x'=2,'z'=4,'y'=4,'c'=2,'t'=2] {'z','y'}, dimensions={0} | all-to-all | bytes 2097152 | tf_op jit(solution)/shard_map/all_to_all | solution.py:830
  108.8 25.4 %collective-permute-start.20 = (bf16[4096,128]{1,0:T(8,128)(2,1)S(1)}, bf16[4096,128]{1,0:T(8,128)(2,1)S(1)}, u32[]{:S(2)}, u32[]{:S(2)}) collective-permute-start(bf16[4096,128]{1,0:T(8,128)(2,1)S(1)} %bitcast.40), channel_id=1, source_target_pairs={{2,0},{0,2},{3,1},{1,3},{6,4},{4,6},{7,5},{5,7},{10,8},{8,10},{11,... | collective-permute-start | bytes 3145736 | tf_op jit(solution)/shard_map/ppermute | solution.py:22
  141.0 10.7 %attend.1 = (f32[8,128,256]{2,1,0:T(8,128)S(1)}, f32[8,1,256]{2,1,0:T(1,128)S(1)}) custom-call(s32[4]{0:T(128)S(1)} %copy-done.41, s32[2,4]{1,0:T(2,128)S(1)} %copy-done.43, bf16[8,128,256]{2,1,0:T(8,128)(2,1)S(1)} %pad_maximum_fusion.2.qt_ref, bf16[4096,128]{1,0:T(8,128)(2,1)S(1)} %get-tuple-element.118.k_ref, bf16[128,4096]{1,0:T(8,128)(2,1)S(1)} %get-tuple-element.119.vt_ref), custom_call_target="tpu_custom_call" | custom-call | flops 1024 | bytes 1024 | tf_op jit(solution)/shard_map/attend/pallas_call | solution.py:607
  156.2 3.0 collective-permute-start.22
  159.8 11.4 %collective-permute-done.22 = bf16[128,2048]{1,0:T(8,128)(2,1)S(1)} collective-permute-done((bf16[128,2048]{1,0:T(8,128)(2,1)S(1)}, bf16[128,2048]{1,0:T(8,128)(2,1)S(1)}, u32[]{:S(2)}, u32[]{:S(2)}) %collective-permute-start.22) | collective-permute-done | bytes 524320 | tf_op jit(solution)/shard_map/ppermute | solution.py:22
  177.6 29.0 %feed_forward.1 = (bf16[2048,4224]{1,0:T(8,128)(2,1)}, bf16[128,2048]{1,0:T(8,128)(2,1)}, bf16[128,2048]{1,0:T(8,128)(2,1)}, bf16[128,2048]{1,0:T(8,128)(2,1)}, bf16[128,2048]{1,0:T(8,128)(2,1)}) custom-call(s32[4]{0:T(128)} %pad_add_fusion.pos_ref, bf16[2048,256]{1,0:T(8,128)(2,1)} %bitcast.39, bf16[2048,256]{1,0:T(8,128)(2,1)} %bitcast.38, ...), custom_call_target="tpu_custom_call" | custom-call | flops 1024 | bytes 1024 | tf_op jit(solution)/shard_map/feed_forward/pallas_call | solution.py:327
  210.1 3.0 collective-permute-start.25
  213.0 11.8 %collective-permute-done.25 = bf16[128,2048]{1,0:T(8,128)(2,1)S(1)} collective-permute-done((bf16[128,2048]{1,0:T(8,128)(2,1)S(1)}, bf16[128,2048]{1,0:T(8,128)(2,1)S(1)}, u32[]{:S(2)}, u32[]{:S(2)}) %collective-permute-start.25) | collective-permute-done | bytes 524320 | tf_op jit(solution)/shard_map/ppermute | solution.py:22
  234.1 7.9 %attend_back.1 = (f32[8,128,256]{2,1,0:T(8,128)S(1)}, f32[4096,128]{1,0:T(8,128)S(1)}, bf16[4096,128]{1,0:T(8,128)(2,1)S(1)}) custom-call(s32[4]{0:T(128)S(1)} %copy-done.42, s32[2,4]{1,0:T(2,128)S(1)} %copy-done.43, bf16[8,128,256]{2,1,0:T(8,128)(2,1)S(1)} %copy-done.16, bf16[8,128,256]{2,1,0:T(8,128)(2,1)S(1)} %pad_maximum_fusion.3.dot_ref, ...), custom_call_target="tpu_custom_call" | custom-call | flops 1024 | bytes 1024 | tf_op jit(solution)/shard_map/attend_back/pallas_call | solution.py:692
  243.7 3.0 weight_chunks.1
  247.9 3.0 collective-permute-start.29
  252.2 30.4 %all-to-all-start.1 = ((bf16[16,256,128]{2,1,0:T(8,128)(2,1)}), bf16[16,256,128]{2,1,0:T(8,128)(2,1)}, u32[]{:S(2)}, u32[]{:S(2)}) async-start(bf16[16,256,128]{2,1,0:T(8,128)(2,1)} %bitcast.49), calls=%async_computation.1 | async-start | bytes 2097152 | tf_op jit(solution)/shard_map/all_to_all | solution.py:875
  290.4 28.1 %collective-permute-done.30 = bf16[256,1024]{1,0:T(8,128)(2,1)} collective-permute-done((bf16[256,1024]{1,0:T(8,128)(2,1)}, bf16[256,1024]{1,0:T(8,128)(2,1)}, u32[]{:S(2)}, u32[]{:S(2)}) %collective-permute-start.30) | collective-permute-done | bytes 524320 | tf_op jit(solution)/shard_map/ppermute | solution.py:22
  327.1 2.9 collective-permute-start.35
  339.1 4.8 %all-to-all-start.2 = ((bf16[32,2,32,256]{3,2,1,0:T(8,128)(2,1)}), bf16[32,2,32,256]{3,2,1,0:T(8,128)(2,1)}, u32[]{:S(2)}, u32[]{:S(2)}) async-start(bf16[32,2,32,256]{3,2,1,0:T(8,128)(2,1)} %bitcast.24), calls=%async_computation.2 | async-start | bytes 2097152 | tf_op jit(solution)/shard_map/all_to_all | solution.py:892
  345.6 2.6 fusion.2
  348.3 15.0 %collective-permute-done.36 = bf16[256,1024]{1,0:T(8,128)(2,1)} collective-permute-done((bf16[256,1024]{1,0:T(8,128)(2,1)S(1)}, bf16[256,1024]{1,0:T(8,128)(2,1)}, u32[]{:S(2)}, u32[]{:S(2)}) %collective-permute-start.36) | collective-permute-done | bytes 524320 | tf_op jit(solution)/shard_map/ppermute | solution.py:22
  364.3 5.9 %all-to-all-done.2 = bf16[32,2,32,256]{3,2,1,0:T(8,128)(2,1)} async-done(((bf16[32,2,32,256]{3,2,1,0:T(8,128)(2,1)}), bf16[32,2,32,256]{3,2,1,0:T(8,128)(2,1)}, u32[]{:S(2)}, u32[]{:S(2)}) %all-to-all-start.2) | async-done | bytes 1048608 | tf_op jit(solution)/shard_map/all_to_all | solution.py:892
  385.2 2.7 collective-permute-start.39
  391.3 10.2 %collective-permute-done.46 = bf16[64,4224]{1,0:T(8,128)(2,1)S(1)} collective-permute-done((bf16[64,4224]{1,0:T(8,128)(2,1)S(1)}, bf16[64,4224]{1,0:T(8,128)(2,1)S(1)}, u32[]{:S(2)}, u32[]{:S(2)}) %collective-permute-start.46) | collective-permute-done | bytes 540704 | tf_op jit(solution)/shard_map/ppermute | solution.py:22
  405.5 2.6 collective-permute-start.48
  (333 shorter events, 121.6 us)
Async XLA Ops:
  7.2 170.4 %all-gather.2.cloned.1.call-start = ((), (), s32[]{:S(2)}) async-start(), calls=%async_computation.4 | async-start | bytes 18382848 | tf_op jit(solution)/shard_map/all_gather | solution.py:801
  17.0 21.0 %collective-permute-start.4 = (bf16[64,4224]{1,0:T(8,128)(2,1)S(1)}, bf16[64,4224]{1,0:T(8,128)(2,1)S(1)}, u32[]{:S(2)}, u32[]{:S(2)}) collective-permute-start(bf16[64,4224]{1,0:T(8,128)(2,1)S(1)} %pad_maximum_fusion.1), channel_id=1, source_target_pairs={{64,0},{0,64},{65,1},{1,65},{66,2},{2,66},{67,3},{3,67},{68,4},{4,... | collective-permute-start | bytes 1622024 | tf_op jit(solution)/shard_map/ppermute | solution.py:22
  20.2 9.6 %collective-permute-start.10 = (bf16[64,1280]{1,0:T(8,128)(2,1)S(1)}, bf16[64,1280]{1,0:T(8,128)(2,1)S(1)}, u32[]{:S(2)}, u32[]{:S(2)}) collective-permute-start(bf16[64,1280]{1,0:T(8,128)(2,1)S(1)} %pad_maximum_fusion.7), channel_id=1, source_target_pairs={{8,0},{12,4},{0,8},{4,12},{9,1},{13,5},{1,9},{5,13},{10,2},{14,6},... | collective-permute-start | bytes 491528 | tf_op jit(solution)/shard_map/ppermute | solution.py:22
  23.7 9.0 %collective-permute-start.9 = (bf16[64,1280]{1,0:T(8,128)(2,1)S(1)}, bf16[64,1280]{1,0:T(8,128)(2,1)S(1)}, u32[]{:S(2)}, u32[]{:S(2)}) collective-permute-start(bf16[64,1280]{1,0:T(8,128)(2,1)S(1)} %pad_maximum_fusion.7), channel_id=1, source_target_pairs={{4,0},{8,4},{12,8},{0,12},{5,1},{9,5},{13,9},{1,13},{6,2},{10,6},{... | collective-permute-start | bytes 491528 | tf_op jit(solution)/shard_map/ppermute | solution.py:22
  39.2 343.6 %reduce-scatter.2.cloned.1.call-start = ((), (), s32[]{:S(2)}) async-start(), calls=%async_computation.5 | async-start | bytes 18382848 | tf_op jit(solution)/shard_map/reduce_scatter | solution.py:846
  39.3 14.3 %collective-permute-start.14 = (bf16[256,1280]{1,0:T(8,128)(2,1)S(1)}, bf16[256,1280]{1,0:T(8,128)(2,1)S(1)}, u32[]{:S(2)}, u32[]{:S(2)}) collective-permute-start(bf16[256,1280]{1,0:T(8,128)(2,1)S(1)} %constant_dynamic-update-slice_fusion.4.refs_4_.refs_12_.refs_5_.refs_6_.refs_14_), channel_id=1, source_target_pairs={{16,0},{32,16},{48,32},{0,48},{17,1},{33,17},{49,33},{1,49},{18,2}... | collective-permute-start | bytes 1966088 | tf_op jit(solution)/shard_map/ppermute | solution.py:22
  42.0 14.8 %collective-permute-start.15 = (bf16[256,1280]{1,0:T(8,128)(2,1)S(1)}, bf16[256,1280]{1,0:T(8,128)(2,1)S(1)}, u32[]{:S(2)}, u32[]{:S(2)}) collective-permute-start(bf16[256,1280]{1,0:T(8,128)(2,1)S(1)} %constant_dynamic-update-slice_fusion.4.refs_4_.refs_12_.refs_5_.refs_6_.refs_14_), channel_id=1, source_target_pairs={{48,0},{0,16},{16,32},{32,48},{49,1},{1,17},{17,33},{33,49},{50,2}... | collective-permute-start | bytes 1966088 | tf_op jit(solution)/shard_map/ppermute | solution.py:22
  44.8 16.0 %collective-permute-start.12 = (bf16[256,1280]{1,0:T(8,128)(2,1)}, bf16[256,1280]{1,0:T(8,128)(2,1)S(1)}, u32[]{:S(2)}, u32[]{:S(2)}) collective-permute-start(bf16[256,1280]{1,0:T(8,128)(2,1)} %constant_dynamic-update-slice_fusion.refs_0_.refs_8_.refs_1_.refs_2_.refs_10_), channel_id=1, source_target_pairs={{4,0},{8,4},{12,8},{0,12},{5,1},{9,5},{13,9},{1,13},{6,2},{10,6},{... | collective-permute-start | bytes 1966088 | tf_op jit(solution)/shard_map/ppermute | solution.py:22
  44.8 16.4 %collective-permute-start.13 = (bf16[256,1280]{1,0:T(8,128)(2,1)}, bf16[256,1280]{1,0:T(8,128)(2,1)S(1)}, u32[]{:S(2)}, u32[]{:S(2)}) collective-permute-start(bf16[256,1280]{1,0:T(8,128)(2,1)} %constant_dynamic-update-slice_fusion.refs_0_.refs_8_.refs_1_.refs_2_.refs_10_), channel_id=1, source_target_pairs={{12,0},{0,4},{4,8},{8,12},{13,1},{1,5},{5,9},{9,13},{14,2},{2,6},{... | collective-permute-start | bytes 1966088 | tf_op jit(solution)/shard_map/ppermute | solution.py:22
  61.2 14.1 %collective-permute-start.18 = (bf16[128,1280]{1,0:T(8,128)(2,1)S(1)}, bf16[128,1280]{1,0:T(8,128)(2,1)S(1)}, u32[]{:S(2)}, u32[]{:S(2)}) collective-permute-start(bf16[128,1280]{1,0:T(8,128)(2,1)S(1)} %slice.222), channel_id=1, source_target_pairs={{16,0},{32,16},{48,32},{0,48},{17,1},{33,17},{49,33},{1,49},{18,2}... | collective-permute-start | bytes 983048 | tf_op jit(solution)/shard_map/ppermute | solution.py:22
  64.3 15.6 %collective-permute-start.16 = (bf16[128,1280]{1,0:T(8,128)(2,1)S(1)}, bf16[128,1280]{1,0:T(8,128)(2,1)S(1)}, u32[]{:S(2)}, u32[]{:S(2)}) collective-permute-start(bf16[128,1280]{1,0:T(8,128)(2,1)S(1)} %slice.220), channel_id=1, source_target_pairs={{4,0},{8,4},{12,8},{0,12},{5,1},{9,5},{13,9},{1,13},{6,2},{10,6},{... | collective-permute-start | bytes 983048 | tf_op jit(solution)/shard_map/ppermute | solution.py:22
  65.5 14.4 %collective-permute-start.19 = (bf16[128,1280]{1,0:T(8,128)(2,1)S(1)}, bf16[128,1280]{1,0:T(8,128)(2,1)S(1)}, u32[]{:S(2)}, u32[]{:S(2)}) collective-permute-start(bf16[128,1280]{1,0:T(8,128)(2,1)S(1)} %slice.223), channel_id=1, source_target_pairs={{48,0},{0,16},{16,32},{32,48},{49,1},{1,17},{17,33},{33,49},{50,2}... | collective-permute-start | bytes 983048 | tf_op jit(solution)/shard_map/ppermute | solution.py:22
  65.6 16.5 %collective-permute-start.17 = (bf16[128,1280]{1,0:T(8,128)(2,1)S(1)}, bf16[128,1280]{1,0:T(8,128)(2,1)S(1)}, u32[]{:S(2)}, u32[]{:S(2)}) collective-permute-start(bf16[128,1280]{1,0:T(8,128)(2,1)S(1)} %slice.221), channel_id=1, source_target_pairs={{12,0},{0,4},{4,8},{8,12},{13,1},{1,5},{5,9},{9,13},{14,2},{2,6},{... | collective-permute-start | bytes 983048 | tf_op jit(solution)/shard_map/ppermute | solution.py:22
  108.8 28.5 %collective-permute-start.20 = (bf16[4096,128]{1,0:T(8,128)(2,1)S(1)}, bf16[4096,128]{1,0:T(8,128)(2,1)S(1)}, u32[]{:S(2)}, u32[]{:S(2)}) collective-permute-start(bf16[4096,128]{1,0:T(8,128)(2,1)S(1)} %bitcast.40), channel_id=1, source_target_pairs={{2,0},{0,2},{3,1},{1,3},{6,4},{4,6},{7,5},{5,7},{10,8},{8,10},{11,... | collective-permute-start | bytes 3145736 | tf_op jit(solution)/shard_map/ppermute | solution.py:22
  156.2 15.0 %collective-permute-start.22 = (bf16[128,2048]{1,0:T(8,128)(2,1)S(1)}, bf16[128,2048]{1,0:T(8,128)(2,1)S(1)}, u32[]{:S(2)}, u32[]{:S(2)}) collective-permute-start(bf16[128,2048]{1,0:T(8,128)(2,1)S(1)} %add_convert_fusion.4), channel_id=1, source_target_pairs={{1,0},{0,1},{3,2},{2,3},{5,4},{4,5},{7,6},{6,7},{9,8},{8,9},{11,10... | collective-permute-start | bytes 1572872 | tf_op jit(solution)/shard_map/ppermute | solution.py:22
  210.1 14.7 %collective-permute-start.25 = (bf16[128,2048]{1,0:T(8,128)(2,1)S(1)}, bf16[128,2048]{1,0:T(8,128)(2,1)S(1)}, u32[]{:S(2)}, u32[]{:S(2)}) collective-permute-start(bf16[128,2048]{1,0:T(8,128)(2,1)S(1)} %add_convert_fusion.3), channel_id=1, source_target_pairs={{1,0},{0,1},{3,2},{2,3},{5,4},{4,5},{7,6},{6,7},{9,8},{8,9},{11,10... | collective-permute-start | bytes 1572872 | tf_op jit(solution)/shard_map/ppermute | solution.py:22
  247.9 40.1 %collective-permute-start.29 = (bf16[128,2048]{1,0:T(8,128)(2,1)}, bf16[128,2048]{1,0:T(8,128)(2,1)}, u32[]{:S(2)}, u32[]{:S(2)}) collective-permute-start(bf16[128,2048]{1,0:T(8,128)(2,1)} %add_convert_fusion.2), channel_id=1, source_target_pairs={{1,0},{0,1},{3,2},{2,3},{5,4},{4,5},{7,6},{6,7},{9,8},{8,9},{11,10... | collective-permute-start | bytes 1572872 | tf_op jit(solution)/shard_map/ppermute | solution.py:22
  252.2 66.3 %all-to-all-start.1 = ((bf16[16,256,128]{2,1,0:T(8,128)(2,1)}), bf16[16,256,128]{2,1,0:T(8,128)(2,1)}, u32[]{:S(2)}, u32[]{:S(2)}) async-start(bf16[16,256,128]{2,1,0:T(8,128)(2,1)} %bitcast.49), calls=%async_computation.1 | async-start | bytes 2097152 | tf_op jit(solution)/shard_map/all_to_all | solution.py:875
  282.6 35.8 %collective-permute-start.30 = (bf16[256,1024]{1,0:T(8,128)(2,1)}, bf16[256,1024]{1,0:T(8,128)(2,1)}, u32[]{:S(2)}, u32[]{:S(2)}) collective-permute-start(bf16[256,1024]{1,0:T(8,128)(2,1)} %copy-done.53), channel_id=1, source_target_pairs={{12,0},{0,4},{4,8},{8,12},{13,1},{1,5},{5,9},{9,13},{14,2},{2,6},{... | collective-permute-start | bytes 1572872 | tf_op jit(solution)/shard_map/ppermute | solution.py:22
  283.9 34.5 %collective-permute-start.31 = (bf16[256,1024]{1,0:T(8,128)(2,1)}, bf16[256,1024]{1,0:T(8,128)(2,1)}, u32[]{:S(2)}, u32[]{:S(2)}) collective-permute-start(bf16[256,1024]{1,0:T(8,128)(2,1)} %copy-done.52), channel_id=1, source_target_pairs={{4,0},{8,4},{12,8},{0,12},{5,1},{9,5},{13,9},{1,13},{6,2},{10,6},{... | collective-permute-start | bytes 1572872 | tf_op jit(solution)/shard_map/ppermute | solution.py:22
  285.4 33.1 %collective-permute-start.32 = (bf16[256,1024]{1,0:T(8,128)(2,1)}, bf16[256,1024]{1,0:T(8,128)(2,1)}, u32[]{:S(2)}, u32[]{:S(2)}) collective-permute-start(bf16[256,1024]{1,0:T(8,128)(2,1)} %copy-done.51), channel_id=1, source_target_pairs={{48,0},{0,16},{16,32},{32,48},{49,1},{1,17},{17,33},{33,49},{50,2}... | collective-permute-start | bytes 1572872 | tf_op jit(solution)/shard_map/ppermute | solution.py:22
  286.6 31.8 %collective-permute-start.33 = (bf16[256,1024]{1,0:T(8,128)(2,1)}, bf16[256,1024]{1,0:T(8,128)(2,1)}, u32[]{:S(2)}, u32[]{:S(2)}) collective-permute-start(bf16[256,1024]{1,0:T(8,128)(2,1)} %copy-done.50), channel_id=1, source_target_pairs={{16,0},{32,16},{48,32},{0,48},{17,1},{33,17},{49,33},{1,49},{18,2}... | collective-permute-start | bytes 1572872 | tf_op jit(solution)/shard_map/ppermute | solution.py:22
  327.1 16.8 %collective-permute-start.35 = (bf16[128,2048]{1,0:T(8,128)(2,1)}, bf16[128,2048]{1,0:T(8,128)(2,1)}, u32[]{:S(2)}, u32[]{:S(2)}) collective-permute-start(bf16[128,2048]{1,0:T(8,128)(2,1)} %add_convert_fusion.1), channel_id=1, source_target_pairs={{1,0},{0,1},{3,2},{2,3},{5,4},{4,5},{7,6},{6,7},{9,8},{8,9},{11,10... | collective-permute-start | bytes 1572872 | tf_op jit(solution)/shard_map/ppermute | solution.py:22
  332.0 31.3 %collective-permute-start.36 = (bf16[256,1024]{1,0:T(8,128)(2,1)S(1)}, bf16[256,1024]{1,0:T(8,128)(2,1)}, u32[]{:S(2)}, u32[]{:S(2)}) collective-permute-start(bf16[256,1024]{1,0:T(8,128)(2,1)S(1)} %copy-done.49), channel_id=1, source_target_pairs={{8,0},{12,4},{0,8},{4,12},{9,1},{13,5},{1,9},{5,13},{10,2},{14,6},... | collective-permute-start | bytes 1572872 | tf_op jit(solution)/shard_map/ppermute | solution.py:22
  334.5 29.8 %collective-permute-start.37 = (bf16[256,1024]{1,0:T(8,128)(2,1)S(1)}, bf16[256,1024]{1,0:T(8,128)(2,1)}, u32[]{:S(2)}, u32[]{:S(2)}) collective-permute-start(bf16[256,1024]{1,0:T(8,128)(2,1)S(1)} %copy-done.47), channel_id=1, source_target_pairs={{32,0},{48,16},{0,32},{16,48},{33,1},{49,17},{1,33},{17,49},{34,2}... | collective-permute-start | bytes 1572872 | tf_op jit(solution)/shard_map/ppermute | solution.py:22
  339.1 31.0 %all-to-all-start.2 = ((bf16[32,2,32,256]{3,2,1,0:T(8,128)(2,1)}), bf16[32,2,32,256]{3,2,1,0:T(8,128)(2,1)}, u32[]{:S(2)}, u32[]{:S(2)}) async-start(bf16[32,2,32,256]{3,2,1,0:T(8,128)(2,1)} %bitcast.24), calls=%async_computation.2 | async-start | bytes 2097152 | tf_op jit(solution)/shard_map/all_to_all | solution.py:892
  371.7 12.1 %collective-permute-start.40 = (bf16[64,1024]{1,0:T(8,128)(2,1)S(1)}, bf16[64,1024]{1,0:T(8,128)(2,1)S(1)}, u32[]{:S(2)}, u32[]{:S(2)}) collective-permute-start(bf16[64,1024]{1,0:T(8,128)(2,1)S(1)} %get-tuple-element.192), channel_id=1, source_target_pairs={{48,0},{0,16},{16,32},{32,48},{49,1},{1,17},{17,33},{33,49},{50,2}... | collective-permute-start | bytes 393224 | tf_op jit(solution)/shard_map/ppermute | solution.py:22
  373.1 12.1 %collective-permute-start.41 = (bf16[64,1024]{1,0:T(8,128)(2,1)S(1)}, bf16[64,1024]{1,0:T(8,128)(2,1)S(1)}, u32[]{:S(2)}, u32[]{:S(2)}) collective-permute-start(bf16[64,1024]{1,0:T(8,128)(2,1)S(1)} %get-tuple-element.194), channel_id=1, source_target_pairs={{32,0},{48,16},{0,32},{16,48},{33,1},{49,17},{1,33},{17,49},{34,2}... | collective-permute-start | bytes 393224 | tf_op jit(solution)/shard_map/ppermute | solution.py:22
  373.8 14.1 %collective-permute-start.42 = (bf16[64,1024]{1,0:T(8,128)(2,1)S(1)}, bf16[64,1024]{1,0:T(8,128)(2,1)S(1)}, u32[]{:S(2)}, u32[]{:S(2)}) collective-permute-start(bf16[64,1024]{1,0:T(8,128)(2,1)S(1)} %get-tuple-element.193), channel_id=1, source_target_pairs={{16,0},{32,16},{48,32},{0,48},{17,1},{33,17},{49,33},{1,49},{18,2}... | collective-permute-start | bytes 393224 | tf_op jit(solution)/shard_map/ppermute | solution.py:22
  380.7 9.2 %collective-permute-start.43 = (bf16[64,1024]{1,0:T(8,128)(2,1)S(1)}, bf16[64,1024]{1,0:T(8,128)(2,1)S(1)}, u32[]{:S(2)}, u32[]{:S(2)}) collective-permute-start(bf16[64,1024]{1,0:T(8,128)(2,1)S(1)} %get-tuple-element.195), channel_id=1, source_target_pairs={{12,0},{0,4},{4,8},{8,12},{13,1},{1,5},{5,9},{9,13},{14,2},{2,6},{... | collective-permute-start | bytes 393224 | tf_op jit(solution)/shard_map/ppermute | solution.py:22
  385.2 22.9 %collective-permute-start.39 = (f32[32,384]{1,0:T(8,128)S(1)}, f32[32,384]{1,0:T(8,128)S(1)}, u32[]{:S(2)}, u32[]{:S(2)}) collective-permute-start(f32[32,384]{1,0:T(8,128)S(1)} %pad_maximum_fusion.9), channel_id=1, source_target_pairs={{1,0},{0,1},{3,2},{2,3},{5,4},{4,5},{7,6},{6,7},{9,8},{8,9},{11,10... | collective-permute-start | bytes 147464 | tf_op jit(solution)/shard_map/ppermute | solution.py:22
  387.9 13.7 %collective-permute-start.46 = (bf16[64,4224]{1,0:T(8,128)(2,1)S(1)}, bf16[64,4224]{1,0:T(8,128)(2,1)S(1)}, u32[]{:S(2)}, u32[]{:S(2)}) collective-permute-start(bf16[64,4224]{1,0:T(8,128)(2,1)S(1)} %slice.305), channel_id=1, source_target_pairs={{64,0},{0,64},{65,1},{1,65},{66,2},{2,66},{67,3},{3,67},{68,4},{4,... | collective-permute-start | bytes 1622024 | tf_op jit(solution)/shard_map/ppermute | solution.py:22
  (98 other events, 947.7 us)
Sparse Core Ops, SparseCore 0:
  39.3 136.2 all-gather.1
  206.8 163.4 reduce-scatter.1
